TPU v7x, 32 devices: a whole 2x2x4 slice. The times are simulated.
32 devices in a mesh: ctx: 8 (over y, x, core), head: 4 (over z).
Axes of the slice: x: 2, y: 2, z: 4, core: 2. Of those that a mesh axis runs over, the one named last changes fastest.
Arguments:
- packets: float32 [2048, 1024], P('ctx', 'head')
- baseline: float32 [2048, 1024], P('ctx', 'head'), may hold values from -3 to 3
- w_query: float32 [1024, 1024], P('head'), may hold values from -0.1875 to 0.1875
- w_key: float32 [1024, 1024], P('head'), may hold values from -0.1875 to 0.1875
- w_value: float32 [1024, 1024], P('head'), may hold values from -0.1875 to 0.1875
- w_out: float32 [1024, 1024], P('head'), may hold values from -0.1875 to 0.1875
- gain: float32 [1024], P('head'), may hold values from 0.1 to 1.9
- probe: float32 [2048, 1024], P('ctx', 'head'), may hold values from -6 to 6
- sessions: int32 [2048], replicated, may hold values from 0 to 3, never falling along the last dimension, each value on 1 to 1024 neighbouring positions
- block_lists: int32 [16, 5], P('ctx'), may hold values from 0 to 15, as said below
Outputs:
- attributions: float32 [2048, 1024], P('ctx', 'head')
Inputs may be any that keep to these rules, and one draw needn't show every extreme that they name: `block_lists`: row b lists 5 different blocks, b itself first, all within 4 blocks of b.
All inputs are finite; a program needn't handle non-finite values.
Results may differ from a plain program's by a relative error of at most 0.0003.
Values sent between devices are 32-bit elements; how exact they have to be, the bound alone decides.
No kernel may reach another device: no remote copies, remote signals or barrier semaphores. Data moves between devices by JAX's collectives and lax.ppermute only.
A program may use at most 128 MiB of HBM per device.

v0:
```python
import functools
import math

import jax
import jax.numpy as jnp
from jax import lax
from jax.experimental import pallas as pl
from jax.experimental.pallas import tpu as pltpu
from jax.sharding import PartitionSpec as P

HEADS = 16
BLK = 128
KVB = 5
REACH = 2


ALPHAS = (0.25, 0.75)
EPS = 1e-05
HIGHEST = lax.Precision.HIGHEST


def from_behind(x, axis, by):
    size = lax.axis_size(axis)
    pairs = [(i, i + by) for i in range(size) if 0 <= i + by < size]
    return lax.ppermute(x, axis, pairs)


def integrate(points, weights_qkv, w_out, gain, probe, sessions, block_lists):
    steps, rows, feats = points.shape
    width = weights_qkv.shape[1]
    head_dim = width // HEADS
    local_heads = feats // head_dim
    blocks = rows // BLK
    where = lax.axis_index("ctx")
    first = (where - REACH) * blocks
    slots = (2 * REACH + 1) * blocks
    scale = 1.0 / math.sqrt(head_dim)
    part_cols = weights_qkv
    qkv = jnp.einsum(
        "std,ed->ste",
        lax.all_gather(points, "head", axis=2, tiled=True),
        part_cols,
        precision=HIGHEST,
    )
    query = qkv[:, :, :feats]
    pairs = qkv[:, :, feats:]
    below = []
    above = []
    for dist in range(1, REACH + 1):
        below.append(from_behind(pairs, "ctx", dist))
        above.append(from_behind(pairs, "ctx", -dist))
    window = jnp.concatenate(below[::-1] + [pairs] + above, axis=1)
    local = (block_lists - first).reshape(-1)
    tiles = window.reshape(steps, slots, BLK, 2 * feats)
    picked = jnp.take(tiles, local, axis=1).reshape(
        steps, blocks, KVB * BLK, 2, local_heads, head_dim
    )
    keys = picked[:, :, :, 0]
    values = picked[:, :, :, 1]
    token_index = block_lists[:, :, None] * BLK + jnp.arange(BLK, dtype=jnp.int32)[None, None, :]
    key_sessions = jnp.take(sessions, token_index.reshape(blocks, KVB * BLK), axis=0)
    query_sessions = lax.dynamic_slice_in_dim(sessions, where * rows, rows, 0).reshape(blocks, BLK)
    keep = query_sessions[:, :, None] == key_sessions[:, None, :]
    query_heads = query.reshape(steps, blocks, BLK, local_heads, head_dim)
    scores = jnp.einsum("sbqhd,sbkhd->sbhqk", query_heads, keys, precision=HIGHEST) * scale
    scores = jnp.where(keep[None, :, None], scores, -1e30)
    top = jnp.max(scores, axis=-1, keepdims=True)
    expo = jnp.exp(scores - top)
    probs = expo / jnp.sum(expo, axis=-1, keepdims=True)
    mixed = jnp.einsum("sbhqk,sbkhd->sbqhd", probs, values, precision=HIGHEST)
    heads_out = mixed.reshape(steps, rows, feats)
    part_cols = w_out
    projected = jnp.einsum(
        "std,ed->ste",
        lax.all_gather(heads_out, "head", axis=2, tiled=True),
        part_cols,
        precision=HIGHEST,
    )
    summed = points + projected
    first_sum, second_sum = lax.psum(
        (jnp.sum(summed, axis=-1), jnp.sum(summed * summed, axis=-1)), "head"
    )
    mean = first_sum / width
    inverse = lax.rsqrt(second_sum / width - mean * mean + EPS)
    normed = (summed - mean[..., None]) * inverse[..., None]
    upstream = probe * gain
    upstream_sum, upstream_dot = lax.psum(
        (jnp.sum(upstream, axis=-1), jnp.sum(upstream * normed, axis=-1)), "head"
    )
    direct = inverse[..., None] * (
        upstream - upstream_sum[..., None] / width - normed * (upstream_dot / width)[..., None]
    )
    partial_heads = jnp.einsum("ste,ed->std", direct, w_out, precision=HIGHEST)
    grad_heads = lax.psum_scatter(partial_heads, "head", scatter_dimension=2, tiled=True)
    grad_mixed = grad_heads.reshape(steps, blocks, BLK, local_heads, head_dim)
    delta = jnp.einsum("sbqhd,sbqhd->sbhq", grad_mixed, mixed, precision=HIGHEST)
    grad_probs = jnp.einsum("sbqhd,sbkhd->sbhqk", grad_mixed, values, precision=HIGHEST)
    grad_scores = probs * (grad_probs - delta[..., None]) * scale
    grad_query = jnp.einsum("sbhqk,sbkhd->sbqhd", grad_scores, keys, precision=HIGHEST)
    grad_keys = jnp.einsum("sbhqk,sbqhd->sbkhd", grad_scores, query_heads, precision=HIGHEST)
    grad_values = jnp.einsum("sbhqk,sbqhd->sbkhd", probs, grad_mixed, precision=HIGHEST)
    grad_picked = jnp.stack([grad_keys, grad_values], axis=3).reshape(
        steps, blocks * KVB, BLK, 2 * feats
    )
    selector = (local[:, None] == jnp.arange(slots, dtype=jnp.int32)[None, :]).astype(jnp.float32)
    grad_window = jnp.einsum("snlc,nw->swlc", grad_picked, selector, precision=HIGHEST).reshape(
        steps, slots * BLK, 2 * feats
    )
    owned = grad_window[:, REACH * rows : (REACH + 1) * rows]
    for dist in range(1, REACH + 1):
        upper = grad_window[:, (REACH + dist) * rows : (REACH + dist + 1) * rows]
        lower = grad_window[:, (REACH - dist) * rows : (REACH - dist + 1) * rows]
        owned = owned + from_behind(upper, "ctx", dist)
        owned = owned + from_behind(lower, "ctx", -dist)
    grad_qkv = jnp.concatenate([grad_query.reshape(steps, rows, feats), owned], axis=-1)
    partial_input = jnp.einsum("ste,ed->std", grad_qkv, weights_qkv, precision=HIGHEST)
    return (direct, partial_input)


def collect_inputs(partial_input):
    return lax.psum_scatter(partial_input, "head", scatter_dimension=2, tiled=True)


def general_shards(packets, baseline, w_query, w_key, w_value, w_out, gain, probe, sessions, block_lists):
    weights_qkv = jnp.concatenate([w_query, w_key, w_value], axis=0)
    travel = packets - baseline
    points = jnp.stack([baseline + alpha * travel for alpha in ALPHAS])
    passes = [
        integrate(points[index : index + 1], weights_qkv, w_out, gain, probe, sessions, block_lists)
        for index in range(len(ALPHAS))
    ]
    grads = jnp.zeros_like(packets)
    for direct, partial_input in passes:
        grads = grads + direct.sum(axis=0) + collect_inputs(partial_input).sum(axis=0)
    return travel * grads / len(ALPHAS)


F32 = jnp.float32
BF16 = jnp.bfloat16
MIB = 1 << 20
VM = pl.BlockSpec(memory_space=pltpu.VMEM)
SM = pl.BlockSpec(memory_space=pltpu.SMEM)


def halves(x):
    high = x.astype(BF16)
    low = (x - high.astype(F32)).astype(BF16)
    return high, low


def halves_outside(x):
    rounded = lax.reduce_precision(x, 8, 7)
    return rounded.astype(BF16), (x - rounded).astype(BF16)


def mm(a, b):
    return lax.dot_general(a, b, (((1,), (0,)), ((), ())), preferred_element_type=F32)


def mm_nt(a, b):
    return lax.dot_general(a, b, (((1,), (1,)), ((), ())), preferred_element_type=F32)


def call(kernel, mib, outs, scratch, n_smem, *args, streamed_in=(), streamed_out=(), parked=(), parked_out=False):
    grid = (NBLOCKS // GROUP,) if streamed_in or streamed_out else ()
    one_in = pl.BlockSpec((GROUP, KVB * BLK, BLK), lambda c: (c, 0, 0))
    in_specs = [SM] * n_smem + [VM] * (len(args) - n_smem)
    for i in streamed_in:
        in_specs[i] = one_in
    for i in parked:
        in_specs[i] = pl.BlockSpec(memory_space=pl.ANY)
    args = [
        pltpu.with_memory_space_constraint(x, pltpu.HBM) if i in parked else x
        for i, x in enumerate(args)
    ]
    out_specs = jax.tree.map(
        lambda _: pl.BlockSpec(memory_space=pl.ANY) if parked_out else VM, outs
    )
    if streamed_out:
        out_specs = tuple(one_in if i in streamed_out else VM for i in range(len(outs)))
    return pl.pallas_call(
        kernel,
        out_shape=outs,
        grid=grid,
        in_specs=in_specs,
        out_specs=out_specs,
        scratch_shapes=scratch,
        compiler_params=pltpu.CompilerParams(vmem_limit_bytes=mib * MIB),
    )(*args)


def fetch(sources, places, arrived):
    copies = [
        pltpu.make_async_copy(source, place, arrived.at[i])
        for i, (source, place) in enumerate(zip(sources, places))
    ]
    for copy in copies:
        copy.start()
    return copies


def shift(x, by, low, high):
    return lax.ppermute(x, "head", [(i, i + by) for i in range(low, high + 1)])


def rotate(x, by):
    size = lax.axis_size("head")
    return lax.ppermute(x, "head", [(i, (i + by) % size) for i in range(size)])


def exchange(pieces):
    return [pieces[0]] + [rotate(pieces[k], k) for k in range(1, len(pieces))]


def weights_kernel(w_query, w_key, w_value, high, low):
    for h in range(w_query.shape[0] // HD):
        for i, w in enumerate((w_query, w_key, w_value)):
            at = slice((3 * h + i) * HD, (3 * h + i + 1) * HD)
            high[at], low[at] = halves(w[h * HD : (h + 1) * HD])


def project_kernel(z_ref, w_high, w_low, own, u1, u2, d1, d2, out, rows, x_high, x_low):
    z = z_ref[0]
    n = 4
    quarter, width = rows.shape[1:]
    both, feats = own.shape
    tokens = both // 2
    for k, sources in enumerate(((own,), (u1,), (u2, d2), (d1,))):
        column = pl.multiple_of(lax.rem(z - k + n, n) * feats, feats)
        for s in range(2):
            span = pl.ds(s * tokens, tokens)
            mine = pl.ds(pl.multiple_of(s * tokens + z * quarter, quarter), quarter)
            x = sum(source[span] for source in sources)
            rows[s, :, pl.ds(column, feats)] = sum(source[mine] for source in sources)
            high, low = halves(x)
            x_high[span, pl.ds(column, feats)] = high
            x_low[span, pl.ds(column, feats)] = low
    part = out.shape[1]
    for h in range(n):
        at = slice(h * part, (h + 1) * part)
        r = mm_nt(w_high[at], x_high[...]) + mm_nt(w_low[at], x_high[...])
        r = r + mm_nt(w_high[at], x_low[...])
        for s in range(2):
            out[2 * h + s] = r[:, s * tokens : (s + 1) * tokens]


def project_last_kernel(
    z_ref, w_high, w_low, listed, u3, d3, first, first_rows,
    parked_out, parked_rows, out, rows, left,
):
    z = z_ref[0]
    n = 4
    quarter, width = rows.shape[1:]
    both, feats = u3.shape
    tokens = both // 2
    rows[...] = first_rows[...]
    columns, pieces = [], []
    for k, source in ((1, d3), (3, u3)):
        column = pl.multiple_of(lax.rem(z - k + n, n) * feats, feats)
        for s in range(2):
            mine = pl.ds(pl.multiple_of(s * tokens + z * quarter, quarter), quarter)
            rows[s, :, pl.ds(column, feats)] += source[mine]
        columns.append(pl.ds(column, feats))
        pieces.append(halves(source[...]))
    leaving = [pltpu.make_async_copy(rows, parked_rows, left.at[n])]
    leaving[0].start()
    part = first.shape[1]
    for h in range(n):
        at = slice(h * part, (h + 1) * part)
        r = 0.0
        for column, (high, low) in zip(columns, pieces):
            r = r + mm_nt(w_high[at, column], high) + mm_nt(w_low[at, column], high)
            r = r + mm_nt(w_high[at, column], low)
        for s in range(2):
            out[2 * h + s, :part] = first[2 * h + s] + r[:, s * tokens : (s + 1) * tokens]
            out[2 * h + s, part:] = listed[...]
        pair = pl.ds(2 * h, 2)
        leaving.append(pltpu.make_async_copy(out.at[pair], parked_out.at[pair], left.at[h]))
        leaving[-1].start()
    for copy in leaving:
        copy.wait()


def fold(x):
    top, bottom = x[: HD // 2], x[HD // 2 :]
    left = lax.broadcasted_iota(jnp.int32, top.shape, 1) < HD
    return jnp.where(left, top, pltpu.roll(bottom, HD, 1)), jnp.where(
        left, pltpu.roll(top, HD, 1), bottom
    )


def unfold(first, second):
    left = lax.broadcasted_iota(jnp.int32, first.shape, 1) < HD
    top = jnp.where(left, first, pltpu.roll(second, HD, 1))
    bottom = jnp.where(left, pltpu.roll(first, HD, 1), second)
    return jnp.concatenate([top, bottom], axis=0)


def attend_kernel(
    lists, session_row, qkv, mixed, folded, p_high, p_low, q3, k3, v2, session_col
):
    c = pl.program_id(0)

    @pl.when(c == 0)
    def _():
        columns = session_row[...].T
        for b in range(NBLOCKS):
            t = qkv[b // 2, : 3 * HD, (b % 2) * BLK : (b % 2 + 1) * BLK]
            q_high, q_low = halves(t[:HD] * SCALE)
            session_col[b] = columns[:, b : b + 1]
            q3[b] = jnp.concatenate([q_high, q_high, q_low], axis=0)
            k_high, k_low = halves(t[HD : 2 * HD].T)
            k3[b] = jnp.concatenate([k_high, k_low, k_high], axis=1)
            v_high, v_low = halves(t[2 * HD :])
            v2[b] = jnp.concatenate([v_high, v_low], axis=0)

    blocks = [GROUP * c + e for e in range(GROUP)]
    scores = []
    for b in blocks:
        mine = session_row[pl.ds(b, 1), :]
        tiles = []
        for j in range(KVB):
            other = lists[b, j]
            s = mm(k3[other], q3[b])
            tiles.append(jnp.where(session_col[other] == mine, s, -1e30))
        scores.append(jnp.concatenate(tiles, axis=0))
    tops = [jnp.max(s, axis=0, keepdims=True) for s in scores]
    expos = [jnp.exp(s - top) for s, top in zip(scores, tops)]
    scales = [1.0 / jnp.sum(expo, axis=0, keepdims=True) for expo in expos]
    for b, e, expo, each in zip(blocks, range(GROUP), expos, scales):
        high, low = halves(expo * each)
        p_high[e] = high
        p_low[e] = low
        values = jnp.concatenate([v2[lists[b, j]] for j in range(KVB)], axis=1)
        both = mm(values, high)
        block = both[:HD] + both[HD:] + mm(values[:HD], low)
        mixed[b] = block
        folded[2 * b], folded[2 * b + 1] = fold(block)


def attend_back_kernel(
    lists, qkv, p_high, p_low, grad, mixed, out0, out1, q2, k2, v3, acc
):
    out = (out0, out1)
    c = pl.program_id(0)

    @pl.when(c == 0)
    def _():
        for b in range(NBLOCKS):
            t = qkv[b // 2, : 3 * HD, (b % 2) * BLK : (b % 2 + 1) * BLK]
            q_high, q_low = halves(t[:HD])
            q2[b] = jnp.concatenate([q_high, q_low], axis=0)
            k_high, k_low = halves(t[HD : 2 * HD])
            k2[b] = jnp.concatenate([k_high, k_low], axis=0)
            v_high, v_low = halves(t[2 * HD :].T)
            v3[b] = jnp.concatenate([v_high, v_low, v_high], axis=1)
        acc[...] = jnp.zeros_like(acc)

    blocks = [GROUP * c + e for e in range(GROUP)]
    grads = [unfold(grad[2 * b], grad[2 * b + 1]) for b in blocks]
    parts = [halves(g) for g in grads]
    probs_grads = []
    for b, (g_high, g_low) in zip(blocks, parts):
        g3 = jnp.concatenate([g_high, g_high, g_low], axis=0)
        probs_grads.append(
            jnp.concatenate([mm(v3[lists[b, j]], g3) for j in range(KVB)], axis=0)
        )
    added = []
    for e, b in enumerate(blocks):
        delta = jnp.sum(grads[e] * mixed[b], axis=0, keepdims=True)
        g2 = jnp.concatenate(parts[e], axis=0)
        ph, pw = p_high[e], p_low[e]
        probs = ph.astype(F32) + pw.astype(F32)
        s_high, s_low = halves(probs * (probs_grads[e] - delta) * SCALE)
        keys = jnp.concatenate([k2[lists[b, j]] for j in range(KVB)], axis=1)
        both = mm(keys, s_high)
        out[e % 2][(GROUP // 2) * c + e // 2, 0:HD] = (
            both[:HD] + both[HD:] + mm(keys[:HD], s_low)
        )
        query = q2[b]
        both = mm_nt(query, s_high)
        grad_keys = both[:HD] + both[HD:] + mm_nt(query[:HD], s_low)
        both = mm_nt(g2, ph)
        grad_values = both[:HD] + both[HD:] + mm_nt(g2[:HD], pw)
        added.append(jnp.concatenate([grad_keys, grad_values], axis=0))
    for b, both in zip(blocks, added):
        for j in range(KVB):
            acc[lists[b, j]] += both[:, j * BLK : (j + 1) * BLK]

    @pl.when(c == NBLOCKS // GROUP - 1)
    def _():
        for b in range(NBLOCKS):
            out[b % 2][b // 2, HD : 3 * HD] = acc[b]


def norm_kernel(
    z_ref, parked_whole, parked_rows, u0, u1, u2, u3, pieces, out, direct_sum,
    upstream, mixed, w_high, w_low, rows, whole, arrived,
):
    copies = fetch((parked_rows, parked_whole), (rows, whole), arrived)
    n = 4
    quarter, width = direct_sum.shape
    feats = width // n
    for k, u in enumerate((u0, u1, u2, u3)):
        column = lax.rem(z_ref[0] - k + n, n) * feats
        upstream[:, pl.ds(pl.multiple_of(column, feats), feats)] = u[...]
    for group in range(n):
        for h in range(n):
            at = group * feats + h * HD
            mixed[at : at + HD, :] = unfold(pieces[2 * h * n + group], pieces[(2 * h + 1) * n + group])
    m_high, m_low = halves(mixed[...].T)
    for copy in copies:
        copy.wait()
    for group in range(n):
        at = slice(group * feats, (group + 1) * feats)
        w_high[at], w_low[at] = halves(whole[at])
    projected = mm_nt(m_high, w_high[...]) + mm_nt(m_low, w_high[...]) + mm_nt(m_high, w_low[...])
    summed = rows[...].reshape(2 * quarter, width) + projected
    mean = jnp.sum(summed, axis=-1, keepdims=True) / width
    second = jnp.sum(summed * summed, axis=-1, keepdims=True) / width
    inverse = lax.rsqrt(second - mean * mean + EPS)
    normed = (summed - mean) * inverse
    up = jnp.concatenate([upstream[...], upstream[...]], axis=0)
    up_mean = jnp.sum(up, axis=-1, keepdims=True) / width
    up_dot = jnp.sum(up * normed, axis=-1, keepdims=True) / width
    direct = inverse * (up - up_mean - normed * up_dot)
    direct_sum[...] = direct[:quarter] + direct[quarter:]
    d_high, d_low = halves(direct)
    grad = mm(d_high, w_high[...]) + mm(d_low, w_high[...]) + mm(d_high, w_low[...])
    grad = grad.T
    for group in range(n):
        for h in range(n):
            at = group * feats + h * HD
            out[2 * h * n + group], out[(2 * h + 1) * n + group] = fold(grad[at : at + HD])


def input_kernel(
    half, z_ref, parked_high, parked_low, parked_sum, grads, f0, f1, f2, f3,
    weight_high, weight_low, direct_sum, arrived,
):
    copies = fetch(
        (parked_high, parked_low, parked_sum), (weight_high, weight_low, direct_sum), arrived
    )
    z = z_ref[0]
    n = 4
    quarter, width = direct_sum.shape
    feats = width // n
    g = jnp.concatenate([grads[2 * h] + grads[2 * h + 1] for h in range(n)], axis=0).T
    g_high, g_low = halves(g)
    mine = pl.ds(pl.multiple_of(lax.rem(z, 2) * quarter, quarter), quarter)
    here = z // 2 == half
    for copy in copies:
        copy.wait()
    for k, f in enumerate((f0, f1, f2, f3)):
        column = lax.rem(z + k, n) * feats
        at = pl.ds(pl.multiple_of(column, feats), feats)
        w_high, w_low = weight_high[:, at], weight_low[:, at]
        f[...] = mm(g_high, w_high) + mm(g_low, w_high) + mm(g_high, w_low)
        f[mine, :] += jnp.where(here, direct_sum[:, at], 0.0)


HD = 64
NBLOCKS = 16
GROUP = 4
SCALE = 1.0 / math.sqrt(HD)


def shape(dims, kind=F32):
    return jax.ShapeDtypeStruct(dims, kind)


def in_hbm(dims, kind=F32):
    return pltpu.HBM(dims, kind)


def shards(packets, baseline, w_query, w_key, w_value, w_out, gain, probe, sessions, block_lists):
    tokens, feats = packets.shape
    width = w_query.shape[1]
    n = lax.axis_size("head")
    heads = feats // HD
    members = lax.axis_size("ctx")
    quarter = tokens // n
    z = lax.axis_index("head")
    z_ref = z.reshape(1)
    slab = feats // members
    part = 3 * HD

    travel = packets - baseline
    half = tokens // 2
    own = jnp.concatenate([baseline + alpha * travel for alpha in ALPHAS])
    ups, downs = [own], [own]
    high, low = call(
        weights_kernel, 16, (in_hbm((heads * part, width), BF16),) * 2, [], 0,
        w_query, w_key, w_value,
    )
    slab_rows = lax.dynamic_slice_in_dim(w_out, lax.axis_index("ctx") * slab, slab, 0)
    for step in range(1, n):
        ups.append(shift(ups[-1], 1, step - 1, n - 2))
        downs.append(shift(downs[-1], -1, 1, n - step))
        if step == 1:
            ups[-1], downs[-1], high, low = lax.optimization_barrier(
                (ups[-1], downs[-1], high, low)
            )
        if step == n - 2:
            ups[-1], downs[-1], slab_rows = lax.optimization_barrier(
                (ups[-1], downs[-1], slab_rows)
            )

    whole_out = lax.all_gather(slab_rows, ("head", "ctx"), axis=0, tiled=True)
    listed = block_lists.reshape(1, -1).astype(F32)
    listed = jnp.pad(listed, ((0, 7), (0, tokens - listed.shape[1])))
    first, first_rows = call(
        project_kernel, 20,
        (shape((members, part, tokens)), shape((2, quarter, width))),
        [pltpu.VMEM((2 * tokens, width), BF16)] * 2,
        1, z_ref, high, low, own, ups[1], ups[2], downs[1], downs[2],
    )
    qkv, rows = call(
        project_last_kernel, 20,
        (in_hbm((members, part + 8, tokens)), in_hbm((2, quarter, width))),
        [
            pltpu.VMEM((members, part + 8, tokens), F32),
            pltpu.VMEM((2, quarter, width), F32),
            pltpu.SemaphoreType.DMA((n + 1,)),
        ],
        1, z_ref, high, low, listed, ups[3], downs[3], first, first_rows, parked_out=True,
    )
    qkv, probe = lax.optimization_barrier((qkv, probe))
    qkv = lax.all_to_all(qkv, "ctx", 0, 0, tiled=True)
    upstream = probe * gain
    upstream = exchange(
        [
            lax.dynamic_slice_in_dim(upstream, lax.rem(z + k, n) * quarter, quarter, 0)
            for k in range(n)
        ]
    )
    qkv, upstream = lax.optimization_barrier((qkv, upstream))
    lists = qkv[:, part, : block_lists.size].astype(jnp.int32).reshape(-1, KVB)

    blocks = members * tokens // BLK
    everyone = members * n
    session_row = sessions.astype(F32).reshape(blocks, BLK)
    mixed, folded, p_high, p_low = call(
        attend_kernel, 20,
        (
            in_hbm((blocks, HD, BLK)),
            in_hbm((everyone, HD // 2, BLK)),
            in_hbm((blocks, KVB * BLK, BLK), BF16),
            in_hbm((blocks, KVB * BLK, BLK), BF16),
        ),
        [
            pltpu.VMEM((blocks, part, BLK), BF16),
            pltpu.VMEM((blocks, BLK, part), BF16),
            pltpu.VMEM((blocks, 2 * HD, BLK), BF16),
            pltpu.VMEM((blocks, BLK, 1), F32),
        ],
        1, lists, session_row, qkv, streamed_out=(2, 3),
    )
    folded = lax.all_to_all(folded, ("ctx", "head"), 0, 0, tiled=True)
    grad, direct_sum = call(
        norm_kernel, 24,
        (shape((everyone, HD // 2, BLK)), in_hbm((quarter, width))),
        [
            pltpu.VMEM((quarter, width), F32),
            pltpu.VMEM((width, 2 * quarter), F32),
            pltpu.VMEM((width, width), BF16),
            pltpu.VMEM((width, width), BF16),
            pltpu.VMEM((2, quarter, width), F32),
            pltpu.VMEM((width, width), F32),
            pltpu.SemaphoreType.DMA((2,)),
        ],
        1, z_ref, whole_out, rows, *upstream, folded, parked=(1, 2),
    )
    grad = lax.all_to_all(grad, ("ctx", "head"), 0, 0, tiled=True)
    grad_qkv = call(
        attend_back_kernel, 20,
        (shape((members, part, half)),) * 2,
        [
            pltpu.VMEM((blocks, 2 * HD, BLK), BF16),
            pltpu.VMEM((blocks, 2 * HD, BLK), BF16),
            pltpu.VMEM((blocks, BLK, part), BF16),
            pltpu.VMEM((blocks, 2 * HD, BLK), F32),
        ],
        1, lists, qkv, p_high, p_low, grad, mixed, streamed_in=(2, 3),
    )
    grad_qkv = [lax.all_to_all(g, "ctx", 0, 0, tiled=True) for g in grad_qkv]
    totals = []
    for e in range(2):
        parts = exchange(
            call(
                functools.partial(input_kernel, e), 16,
                (shape((half, feats)),) * n,
                [pltpu.VMEM((heads * part, width), BF16)] * 2
                + [pltpu.VMEM((quarter, width), F32), pltpu.SemaphoreType.DMA((3,))],
                1, z_ref, high, low, direct_sum, grad_qkv[e], parked=(1, 2, 3),
            )
        )
        totals.append(parts[0] + parts[1] + parts[2] + parts[3])
    return travel * jnp.concatenate(totals) / len(ALPHAS)


def pick_shards(mesh):
    members, n = mesh.shape["ctx"], mesh.shape["head"]
    return shards if n == 4 and members == 2 * HEADS // n else general_shards


def solution(mesh):
    return jax.shard_map(
        pick_shards(mesh),
        mesh=mesh,
        in_specs=(
            P("ctx", "head"),
            P("ctx", "head"),
            P("head", None),
            P("head", None),
            P("head", None),
            P("head", None),
            P("head"),
            P("ctx", "head"),
            P(),
            P("ctx", None),
        ),
        out_specs=P("ctx", "head"),
        check_vma=False,
    )
```

profile of v0, /device:TPU:0, one launch (start us, length us, event | category | flops | bytes accessed | tf_op | source)
XLA Modules:
  0.0 208.7 jit_solution(6554303280510729202)
XLA Ops:
  8.9 1.3 collective-permute-start.1
  10.2 6.4 %collective-permute-start = (f32[512,256]{1,0:T(8,128)S(1)}, f32[512,256]{1,0:T(8,128)}, u32[]{:S(2)}, u32[]{:S(2)}) collective-permute-start(f32[512,256]{1,0:T(8,128)S(1)} %pad_maximum_fusion.own), channel_id=1, source_target_pairs={{0,1},{1,2},{2,3},{4,5},{5,6},{6,7},{8,9},{9,10},{10,11},{12,13},{... | collective-permute-start | bytes 1572872 | tf_op jit(solution)/shard_map/ppermute | solution.py:203
  17.8 2.2 %shard_map.100 = (bf16[768,1024]{1,0:T(8,128)(2,1)}, bf16[768,1024]{1,0:T(8,128)(2,1)}) custom-call(f32[256,1024]{1,0:T(8,128)S(1)} %copy-done.5, f32[256,1024]{1,0:T(8,128)S(1)} %copy-done.6, f32[256,1024]{1,0:T(8,128)S(1)} %copy-done.7), custom_call_target="tpu_custom_call" | custom-call | tf_op jit(solution)/shard_map/pallas_call | solution.py:181
  20.0 5.8 %collective-permute-done.1.d1 = f32[512,256]{1,0:T(8,128)S(1)} collective-permute-done((f32[512,256]{1,0:T(8,128)S(1)}, f32[512,256]{1,0:T(8,128)S(1)}, u32[]{:S(2)}, u32[]{:S(2)}) %collective-permute-start.1) | collective-permute-done | bytes 524320 | tf_op jit(solution)/shard_map/ppermute | solution.py:203
  27.7 1.3 collective-permute-start.3
  29.7 15.9 %collective-permute-done.3.d2 = f32[512,256]{1,0:T(8,128)S(1)} collective-permute-done((f32[512,256]{1,0:T(8,128)S(1)}, f32[512,256]{1,0:T(8,128)S(1)}, u32[]{:S(2)}, u32[]{:S(2)}) %collective-permute-start.3) | collective-permute-done | bytes 524320 | tf_op jit(solution)/shard_map/ppermute | solution.py:203
  45.6 1.5 collective-permute-start.4
  48.5 1.4 copy-done.1
  49.9 1.4 copy-done.2
  51.3 5.2 %shard_map.101 = (f32[8,192,256]{2,1,0:T(8,128)S(1)}, f32[2,64,1024]{2,1,0:T(8,128)S(1)}) custom-call(s32[1]{0:T(128)} %bitcast.z_ref, bf16[768,1024]{1,0:T(8,128)(2,1)S(1)} %copy-done.1, bf16[768,1024]{1,0:T(8,128)(2,1)S(1)} %copy-done.2, f32[512,256]{1,0:T(8,128)S(1)} %pad_maximum_fusion.own, f32[512,256]{1,0:T(8,128)} %collective-permute-done.u1, ...), custom_call_target="tpu_custom_call" | custom-call | tf_op jit(solution)/shard_map/pallas_call | solution.py:181
  56.5 5.9 %collective-permute-done.5.d3 = f32[512,256]{1,0:T(8,128)} collective-permute-done((f32[512,256]{1,0:T(8,128)S(1)}, f32[512,256]{1,0:T(8,128)}, u32[]{:S(2)}, u32[]{:S(2)}) %collective-permute-start.5) | collective-permute-done | bytes 524320 | tf_op jit(solution)/shard_map/ppermute | solution.py:203
  62.5 4.3 %shard_map.102 = (f32[8,200,256]{2,1,0:T(8,128)}, f32[2,64,1024]{2,1,0:T(8,128)}) custom-call(s32[1]{0:T(128)} %bitcast.z_ref, bf16[768,1024]{1,0:T(8,128)(2,1)S(1)} %copy-done.1, bf16[768,1024]{1,0:T(8,128)(2,1)S(1)} %copy-done.2, f32[8,256]{1,0:T(8,128)S(1)} %pad.4.listed, f32[512,256]{1,0:T(8,128)} %collective-permute-done.4.u3, ...), custom_call_target="tpu_custom_call" | custom-call | tf_op jit(solution)/shard_map/pallas_call | solution.py:181
  66.8 4.0 %all-to-all-start = ((f32[8,200,256]{2,1,0:T(8,128)}), f32[8,200,256]{2,1,0:T(8,128)S(1)}, u32[]{:S(2)}, u32[]{:S(2)}) async-start(f32[8,200,256]{2,1,0:T(8,128)} %get-tuple-element.54), calls=%async_computation | async-start | bytes 3276800 | tf_op jit(solution)/shard_map/all_to_all | solution.py:529
  73.0 3.2 %collective-permute-done.8.u3 = f32[64,256]{1,0:T(8,128)S(1)} collective-permute-done((f32[64,256]{1,0:T(8,128)S(1)}, f32[64,256]{1,0:T(8,128)S(1)}, u32[]{:S(2)}, u32[]{:S(2)}) %collective-permute-start.8) | collective-permute-done | bytes 65568 | tf_op jit(solution)/shard_map/ppermute | solution.py:208
  76.2 5.3 %collective-permute-done.7.u2 = f32[64,256]{1,0:T(8,128)S(1)} collective-permute-done((f32[64,256]{1,0:T(8,128)S(1)}, f32[64,256]{1,0:T(8,128)S(1)}, u32[]{:S(2)}, u32[]{:S(2)}) %collective-permute-start.7) | collective-permute-done | bytes 65568 | tf_op jit(solution)/shard_map/ppermute | solution.py:208
  81.5 13.7 %all-to-all-done.qkv = f32[8,200,256]{2,1,0:T(8,128)S(1)} async-done(((f32[8,200,256]{2,1,0:T(8,128)}), f32[8,200,256]{2,1,0:T(8,128)S(1)}, u32[]{:S(2)}, u32[]{:S(2)}) %all-to-all-start) | async-done | bytes 1638432 | tf_op jit(solution)/shard_map/all_to_all | solution.py:529
  95.3 7.4 %shard_map.103 = (f32[16,64,128]{2,1,0:T(8,128)}, f32[32,32,128]{2,1,0:T(8,128)}, bf16[16,640,128]{2,1,0:T(8,128)(2,1)}, bf16[16,640,128]{2,1,0:T(8,128)(2,1)}) custom-call(s32[16,5]{1,0:T(8,128)S(1)} %convert_element_type.29.lists, f32[16,128]{1,0:T(8,128)S(1)} %convert_bitcast_fusion.session_row, f32[8,200,256]{2,1,0:T(8,128)S(1)} %all-to-all-done.qkv), custom_call_target="tpu_custom_call" | custom-call | tf_op jit(solution)/shard_map/pallas_call | solution.py:181
  102.7 17.0 %all_to_all.25.pieces = f32[32,32,128]{2,1,0:T(8,128)S(1)} all-to-all(f32[32,32,128]{2,1,0:T(8,128)} %get-tuple-element.61), channel_id=1, replica_groups=mesh['ctx'=8,'head'=4] {'ctx','head'}, dimensions={0} | all-to-all | bytes 1048576 | tf_op jit(solution)/shard_map/all_to_all | solution.py:559
  119.7 6.4 %shard_map.104 = (f32[32,32,128]{2,1,0:T(8,128)S(1)}, f32[64,1024]{1,0:T(8,128)}) custom-call(s32[1]{0:T(128)} %bitcast.z_ref, f32[1024,1024]{1,0:T(8,128)} %all-gather.2.cloned.1.call-done.parked_whole, f32[2,64,1024]{2,1,0:T(8,128)} %get-tuple-element.52.parked_rows, f32[64,256]{1,0:T(8,128)S(1)} %get-tuple-element.56.u0, ...), custom_call_target="tpu_custom_call" | custom-call | tf_op jit(solution)/shard_map/pallas_call | solution.py:181
  126.1 18.4 %all_to_all.26.grad = f32[32,32,128]{2,1,0:T(8,128)S(1)} all-to-all(f32[32,32,128]{2,1,0:T(8,128)S(1)} %get-tuple-element.65), channel_id=1, replica_groups=mesh['ctx'=8,'head'=4] {'ctx','head'}, dimensions={0} | all-to-all | bytes 1048576 | tf_op jit(solution)/shard_map/all_to_all | solution.py:574
  144.5 9.7 %shard_map.105 = (f32[8,192,128]{2,1,0:T(8,128)}, f32[8,192,128]{2,1,0:T(8,128)S(1)}) custom-call(s32[16,5]{1,0:T(8,128)S(1)} %convert_element_type.29.lists, f32[8,200,256]{2,1,0:T(8,128)S(1)} %all-to-all-done.qkv, bf16[16,640,128]{2,1,0:T(8,128)(2,1)S(1)} %copy-done.3, bf16[16,640,128]{2,1,0:T(8,128)(2,1)S(1)} %copy-done.4, ...), custom_call_target="tpu_custom_call" | custom-call | tf_op jit(solution)/shard_map/pallas_call | solution.py:181
  154.2 15.9 %all_to_all.27.grads = f32[8,192,128]{2,1,0:T(8,128)S(1)} all-to-all(f32[8,192,128]{2,1,0:T(8,128)S(1)} %get-tuple-element.72), channel_id=1, replica_groups=mesh['ctx'=8,'head'=4] {'ctx'}, dimensions={0} | all-to-all | bytes 1572864 | tf_op jit(solution)/shard_map/all_to_all | solution.py:586
  170.1 3.5 %all-to-all-start.3 = ((f32[8,192,128]{2,1,0:T(8,128)}), f32[8,192,128]{2,1,0:T(8,128)S(1)}, u32[]{:S(2)}, u32[]{:S(2)}) async-start(f32[8,192,128]{2,1,0:T(8,128)} %get-tuple-element.67), calls=%async_computation.3 | async-start | bytes 1572864 | tf_op jit(solution)/shard_map/all_to_all | solution.py:586
  173.7 2.8 %shard_map.107 = (f32[128,256]{1,0:T(8,128)S(1)}, f32[128,256]{1,0:T(8,128)S(1)}, f32[128,256]{1,0:T(8,128)S(1)}, f32[128,256]{1,0:T(8,128)S(1)}) custom-call(s32[1]{0:T(128)} %bitcast.z_ref, bf16[768,1024]{1,0:T(8,128)(2,1)} %get-tuple-element.43.w_high.parked_high, bf16[768,1024]{1,0:T(8,128)(2,1)} %get-tuple-element.44.w_low.parked_low, ...), custom_call_target="tpu_custom_call" | custom-call | tf_op jit(solution)/shard_map/pallas_call | solution.py:181
  176.4 1.6 collective-permute-start.12
  179.0 1.5 collective-permute-start.14
  180.5 5.7 %all-to-all-done.3.grads = f32[8,192,128]{2,1,0:T(8,128)S(1)} async-done(((f32[8,192,128]{2,1,0:T(8,128)}), f32[8,192,128]{2,1,0:T(8,128)S(1)}, u32[]{:S(2)}, u32[]{:S(2)}) %all-to-all-start.3) | async-done | bytes 786464 | tf_op jit(solution)/shard_map/all_to_all | solution.py:586
  186.2 2.8 %shard_map.106 = (f32[128,256]{1,0:T(8,128)S(1)}, f32[128,256]{1,0:T(8,128)S(1)}, f32[128,256]{1,0:T(8,128)S(1)}, f32[128,256]{1,0:T(8,128)S(1)}) custom-call(s32[1]{0:T(128)} %bitcast.z_ref, bf16[768,1024]{1,0:T(8,128)(2,1)} %get-tuple-element.43.w_high.parked_high, bf16[768,1024]{1,0:T(8,128)(2,1)} %get-tuple-element.44.w_low.parked_low, ...), custom_call_target="tpu_custom_call" | custom-call | tf_op jit(solution)/shard_map/pallas_call | solution.py:181
  189.0 1.6 collective-permute-start.9
  191.6 1.5 collective-permute-start.11
  193.1 3.1 %collective-permute-done.9 = f32[128,256]{1,0:T(8,128)S(1)} collective-permute-done((f32[128,256]{1,0:T(8,128)S(1)}, f32[128,256]{1,0:T(8,128)S(1)}, u32[]{:S(2)}, u32[]{:S(2)}) %collective-permute-start.9) | collective-permute-done | bytes 131104 | tf_op jit(solution)/shard_map/ppermute | solution.py:208
  196.2 4.9 %collective-permute-done.10 = f32[128,256]{1,0:T(8,128)S(1)} collective-permute-done((f32[128,256]{1,0:T(8,128)S(1)}, f32[128,256]{1,0:T(8,128)S(1)}, u32[]{:S(2)}, u32[]{:S(2)}) %collective-permute-start.10) | collective-permute-done | bytes 131104 | tf_op jit(solution)/shard_map/ppermute | solution.py:208
  (61 shorter events, 12.5 us)
Async XLA Ops:
  6.5 22.4 %copy-start = (f32[256,1024]{1,0:T(8,128)S(1)}, f32[256,1024]{1,0:T(8,128)}, u32[]{:S(2)}) copy-start(f32[256,1024]{1,0:T(8,128)} %param.15) | copy-start | bytes 3145732
  6.5 10.1 %copy-start.5 = (f32[256,1024]{1,0:T(8,128)S(1)}, f32[256,1024]{1,0:T(8,128)}, u32[]{:S(2)}) copy-start(f32[256,1024]{1,0:T(8,128)} %w_query.1) | copy-start | bytes 3145732
  6.5 113.1 %all-gather.2.cloned.1.call-start = ((), (), s32[]{:S(2)}) async-start(), calls=%async_computation.5 | async-start | bytes 4325376 | tf_op jit(solution)/shard_map/all_gather | solution.py:509
  6.5 10.1 %copy-start.6 = (f32[256,1024]{1,0:T(8,128)S(1)}, f32[256,1024]{1,0:T(8,128)}, u32[]{:S(2)}) copy-start(f32[256,1024]{1,0:T(8,128)} %w_key.1) | copy-start | bytes 3145732
  8.9 39.5 %copy-start.14 = (s32[2,5]{1,0:T(2,128)S(1)}, s32[2,5]{1,0:T(2,128)}, u32[]{:S(2)}) copy-start(s32[2,5]{1,0:T(2,128)} %param.19) | copy-start | bytes 124
  8.9 16.8 %collective-permute-start.1 = (f32[512,256]{1,0:T(8,128)S(1)}, f32[512,256]{1,0:T(8,128)S(1)}, u32[]{:S(2)}, u32[]{:S(2)}) collective-permute-start(f32[512,256]{1,0:T(8,128)S(1)} %pad_maximum_fusion.own), channel_id=1, source_target_pairs={{1,0},{2,1},{3,2},{5,4},{6,5},{7,6},{9,8},{10,9},{11,10},{13,12},{... | collective-permute-start | bytes 1572872 | tf_op jit(solution)/shard_map/ppermute | solution.py:203
  10.2 16.7 %collective-permute-start = (f32[512,256]{1,0:T(8,128)S(1)}, f32[512,256]{1,0:T(8,128)}, u32[]{:S(2)}, u32[]{:S(2)}) collective-permute-start(f32[512,256]{1,0:T(8,128)S(1)} %pad_maximum_fusion.own), channel_id=1, source_target_pairs={{0,1},{1,2},{2,3},{4,5},{5,6},{6,7},{8,9},{9,10},{10,11},{12,13},{... | collective-permute-start | bytes 1572872 | tf_op jit(solution)/shard_map/ppermute | solution.py:203
  16.6 1.2 copy-start.7
  27.0 2.7 %collective-permute-start.2 = (f32[512,256]{1,0:T(8,128)}, f32[512,256]{1,0:T(8,128)S(1)}, u32[]{:S(2)}, u32[]{:S(2)}) collective-permute-start(f32[512,256]{1,0:T(8,128)} %collective-permute-done.u1), channel_id=1, source_target_pairs={{1,2},{2,3},{5,6},{6,7},{9,10},{10,11},{13,14},{14,15},{17,18},{18... | collective-permute-start | bytes 1572872 | tf_op jit(solution)/shard_map/ppermute | solution.py:203
  27.7 17.9 %collective-permute-start.3 = (f32[512,256]{1,0:T(8,128)S(1)}, f32[512,256]{1,0:T(8,128)S(1)}, u32[]{:S(2)}, u32[]{:S(2)}) collective-permute-start(f32[512,256]{1,0:T(8,128)S(1)} %collective-permute-done.1.d1), channel_id=1, source_target_pairs={{1,0},{2,1},{5,4},{6,5},{9,8},{10,9},{13,12},{14,13},{17,16},{18,1... | collective-permute-start | bytes 1572872 | tf_op jit(solution)/shard_map/ppermute | solution.py:203
  45.6 10.9 %collective-permute-start.4 = (f32[512,256]{1,0:T(8,128)S(1)}, f32[512,256]{1,0:T(8,128)}, u32[]{:S(2)}, u32[]{:S(2)}) collective-permute-start(f32[512,256]{1,0:T(8,128)S(1)} %collective-permute-done.2.u2), channel_id=1, source_target_pairs={{2,3},{6,7},{10,11},{14,15},{18,19},{22,23},{26,27},{30,31}} | collective-permute-start | bytes 1572872 | tf_op jit(solution)/shard_map/ppermute | solution.py:203
  47.1 15.4 %collective-permute-start.5 = (f32[512,256]{1,0:T(8,128)S(1)}, f32[512,256]{1,0:T(8,128)}, u32[]{:S(2)}, u32[]{:S(2)}) collective-permute-start(f32[512,256]{1,0:T(8,128)S(1)} %collective-permute-done.3.d2), channel_id=1, source_target_pairs={{1,0},{5,4},{9,8},{13,12},{17,16},{21,20},{25,24},{29,28}} | collective-permute-start | bytes 1572872 | tf_op jit(solution)/shard_map/ppermute | solution.py:203
  48.5 1.4 copy-start.1
  49.9 1.4 copy-start.2
  66.7 4.1 %copy-start.11 = (f32[256,256]{1,0:T(8,128)S(1)}, f32[256,256]{1,0:T(8,128)}, u32[]{:S(2)}) copy-start(f32[256,256]{1,0:T(8,128)} %param.17) | copy-start | bytes 786436
  66.7 4.1 %copy-start.13 = (f32[256]{0:T(256)S(1)}, f32[256]{0:T(256)}, u32[]{:S(2)}) copy-start(f32[256]{0:T(256)} %param.16) | copy-start | bytes 3076
  66.8 6.2 %copy-start.12 = (s32[2048]{0:T(1024)S(1)}, s32[2048]{0:T(1024)}, u32[]{:S(2)}) copy-start(s32[2048]{0:T(1024)} %param.18) | copy-start | bytes 24580
  66.8 28.4 %all-to-all-start = ((f32[8,200,256]{2,1,0:T(8,128)}), f32[8,200,256]{2,1,0:T(8,128)S(1)}, u32[]{:S(2)}, u32[]{:S(2)}) async-start(f32[8,200,256]{2,1,0:T(8,128)} %get-tuple-element.54), calls=%async_computation | async-start | bytes 3276800 | tf_op jit(solution)/shard_map/all_to_all | solution.py:529
  70.9 5.3 %collective-permute-start.8 = (f32[64,256]{1,0:T(8,128)S(1)}, f32[64,256]{1,0:T(8,128)S(1)}, u32[]{:S(2)}, u32[]{:S(2)}) collective-permute-start(f32[64,256]{1,0:T(8,128)S(1)} %get-tuple-element.79), channel_id=1, source_target_pairs={{0,3},{1,0},{2,1},{3,2},{4,7},{5,4},{6,5},{7,6},{8,11},{9,8},{10,9... | collective-permute-start | bytes 196616 | tf_op jit(solution)/shard_map/ppermute | solution.py:208
  71.0 10.6 %collective-permute-start.7 = (f32[64,256]{1,0:T(8,128)S(1)}, f32[64,256]{1,0:T(8,128)S(1)}, u32[]{:S(2)}, u32[]{:S(2)}) collective-permute-start(f32[64,256]{1,0:T(8,128)S(1)} %get-tuple-element.80), channel_id=1, source_target_pairs={{0,2},{1,3},{2,0},{3,1},{4,6},{5,7},{6,4},{7,5},{8,10},{9,11},{10,... | collective-permute-start | bytes 196616 | tf_op jit(solution)/shard_map/ppermute | solution.py:208
  71.8 9.7 %collective-permute-start.6 = (f32[64,256]{1,0:T(8,128)S(1)}, f32[64,256]{1,0:T(8,128)S(1)}, u32[]{:S(2)}, u32[]{:S(2)}) collective-permute-start(f32[64,256]{1,0:T(8,128)S(1)} %get-tuple-element.81), channel_id=1, source_target_pairs={{0,1},{1,2},{2,3},{3,0},{4,5},{5,6},{6,7},{7,4},{8,9},{9,10},{10,1... | collective-permute-start | bytes 196616 | tf_op jit(solution)/shard_map/ppermute | solution.py:208
  119.7 24.8 %copy-start.3 = (bf16[16,640,128]{2,1,0:T(8,128)(2,1)S(1)}, bf16[16,640,128]{2,1,0:T(8,128)(2,1)}, u32[]{:S(2)}) copy-start(bf16[16,640,128]{2,1,0:T(8,128)(2,1)} %get-tuple-element.63.p_high) | copy-start | bytes 7864324
  119.7 24.8 %copy-start.4 = (bf16[16,640,128]{2,1,0:T(8,128)(2,1)S(1)}, bf16[16,640,128]{2,1,0:T(8,128)(2,1)}, u32[]{:S(2)}) copy-start(bf16[16,640,128]{2,1,0:T(8,128)(2,1)} %get-tuple-element.64.p_low) | copy-start | bytes 7864324
  119.7 24.8 %copy-start.8 = (f32[16,64,128]{2,1,0:T(8,128)S(1)}, f32[16,64,128]{2,1,0:T(8,128)}, u32[]{:S(2)}) copy-start(f32[16,64,128]{2,1,0:T(8,128)} %get-tuple-element.66.mixed) | copy-start | bytes 1572868
  170.1 16.1 %all-to-all-start.3 = ((f32[8,192,128]{2,1,0:T(8,128)}), f32[8,192,128]{2,1,0:T(8,128)S(1)}, u32[]{:S(2)}, u32[]{:S(2)}) async-start(f32[8,192,128]{2,1,0:T(8,128)} %get-tuple-element.67), calls=%async_computation.3 | async-start | bytes 1572864 | tf_op jit(solution)/shard_map/all_to_all | solution.py:586
  176.4 15.1 %collective-permute-start.12 = (f32[128,256]{1,0:T(8,128)S(1)}, f32[128,256]{1,0:T(8,128)S(1)}, u32[]{:S(2)}, u32[]{:S(2)}) collective-permute-start(f32[128,256]{1,0:T(8,128)S(1)} %get-tuple-element.74), channel_id=1, source_target_pairs={{0,1},{1,2},{2,3},{3,0},{4,5},{5,6},{6,7},{7,4},{8,9},{9,10},{10,1... | collective-permute-start | bytes 393224 | tf_op jit(solution)/shard_map/ppermute | solution.py:208
  178.1 15.0 %collective-permute-start.13 = (f32[128,256]{1,0:T(8,128)S(1)}, f32[128,256]{1,0:T(8,128)S(1)}, u32[]{:S(2)}, u32[]{:S(2)}) collective-permute-start(f32[128,256]{1,0:T(8,128)S(1)} %get-tuple-element.75), channel_id=1, source_target_pairs={{0,2},{1,3},{2,0},{3,1},{4,6},{5,7},{6,4},{7,5},{8,10},{9,11},{10,... | collective-permute-start | bytes 393224 | tf_op jit(solution)/shard_map/ppermute | solution.py:208
  179.0 22.1 %copy-start.10 = (f32[256,256]{1,0:T(8,128)S(1)}, f32[256,256]{1,0:T(8,128)}, u32[]{:S(2)}) copy-start(f32[256,256]{1,0:T(8,128)} %copy-done.9) | copy-start | bytes 786436
  179.0 14.0 %collective-permute-start.14 = (f32[128,256]{1,0:T(8,128)S(1)}, f32[128,256]{1,0:T(8,128)S(1)}, u32[]{:S(2)}, u32[]{:S(2)}) collective-permute-start(f32[128,256]{1,0:T(8,128)S(1)} %get-tuple-element.76), channel_id=1, source_target_pairs={{0,3},{1,0},{2,1},{3,2},{4,7},{5,4},{6,5},{7,6},{8,11},{9,8},{10,9... | collective-permute-start | bytes 393224 | tf_op jit(solution)/shard_map/ppermute | solution.py:208
  189.0 7.3 %collective-permute-start.9 = (f32[128,256]{1,0:T(8,128)S(1)}, f32[128,256]{1,0:T(8,128)S(1)}, u32[]{:S(2)}, u32[]{:S(2)}) collective-permute-start(f32[128,256]{1,0:T(8,128)S(1)} %get-tuple-element.69), channel_id=1, source_target_pairs={{0,1},{1,2},{2,3},{3,0},{4,5},{5,6},{6,7},{7,4},{8,9},{9,10},{10,1... | collective-permute-start | bytes 393224 | tf_op jit(solution)/shard_map/ppermute | solution.py:208
  190.6 10.5 %collective-permute-start.10 = (f32[128,256]{1,0:T(8,128)S(1)}, f32[128,256]{1,0:T(8,128)S(1)}, u32[]{:S(2)}, u32[]{:S(2)}) collective-permute-start(f32[128,256]{1,0:T(8,128)S(1)} %get-tuple-element.70), channel_id=1, source_target_pairs={{0,2},{1,3},{2,0},{3,1},{4,6},{5,7},{6,4},{7,5},{8,10},{9,11},{10,... | collective-permute-start | bytes 393224 | tf_op jit(solution)/shard_map/ppermute | solution.py:208
  191.6 9.5 %collective-permute-start.11 = (f32[128,256]{1,0:T(8,128)S(1)}, f32[128,256]{1,0:T(8,128)S(1)}, u32[]{:S(2)}, u32[]{:S(2)}) collective-permute-start(f32[128,256]{1,0:T(8,128)S(1)} %get-tuple-element.71), channel_id=1, source_target_pairs={{0,3},{1,0},{2,1},{3,2},{4,7},{5,4},{6,5},{7,6},{8,11},{9,8},{10,9... | collective-permute-start | bytes 393224 | tf_op jit(solution)/shard_map/ppermute | solution.py:208
  (1 other events, 1.1 us)
Sparse Core Ops, SparseCore 0:
  45.7 64.3 all-gather.1
where the time goes:
time: 210 us; the launch traced here: 209 us
  waiting for transfers between devices  64.7 us (31%)
  blocking collectives  51.3 us (24%)
  Pallas kernels  40.7 us (19%)
  starting transfers between devices  30.2 us (14%)
  between operations  13.7 us (7%)
  local copies, waits for them, and re-layouts  4.97 us (2%)
  other arithmetic  3.19 us (2%)
    pallas_call x8, Pallas kernels, call(): pl.pallas_call(kernel, out_shape=outs, grid=grid, in_specs=in_specs, out_...  40.7 us
    ppermute x6, waiting for transfers between devices, shift(): return lax.ppermute(x, 'head', [(i, i + by) for i in range(low, high + 1)])  28.8 us
    all_to_all x1, blocking collectives, shards(): grad = lax.all_to_all(grad, ('ctx', 'head'), 0, 0, tiled=True)  18.4 us
    all_to_all x1, blocking collectives, shards(): folded = lax.all_to_all(folded, ('ctx', 'head'), 0, 0, tiled=True)  17 us
    ppermute x9, waiting for transfers between devices, rotate(): return lax.ppermute(x, 'head', [(i, (i + by) % size) for i in range(size)])  16.5 us
    all_to_all x1, blocking collectives, shards(): grad_qkv = [lax.all_to_all(g, 'ctx', 0, 0, tiled=True) for g in grad_qkv]  15.9 us
    all_to_all x1, waiting for transfers between devices, shards(): qkv = lax.all_to_all(qkv, 'ctx', 0, 0, tiled=True)  13.7 us
    ppermute x6, starting transfers between devices, shift(): return lax.ppermute(x, 'head', [(i, i + by) for i in range(low, high + 1)])  12.4 us
  transfers between devices with their start and end apart: 18, of which 10 were waited for; matrix products, arithmetic and copies ran while one was open for 0% of the time, Pallas kernels for 12%

commit v1 on v0

--- a/solution.py
+++ b/solution.py
@@ -397,7 +397,12 @@
     z_ref, parked_whole, parked_rows, u0, u1, u2, u3, pieces, out, direct_sum,
     upstream, mixed, w_high, w_low, rows, whole, arrived,
 ):
-    copies = fetch((parked_rows, parked_whole), (rows, whole), arrived)
+    bands = [pl.ds(group * HD * 4, HD * 4) for group in range(4)]
+    copies = fetch(
+        [parked_whole.at[band] for band in bands] + [parked_rows],
+        [whole.at[band] for band in bands] + [rows],
+        arrived,
+    )
     n = 4
     quarter, width = direct_sum.shape
     feats = width // n
@@ -409,12 +414,15 @@
             at = group * feats + h * HD
             mixed[at : at + HD, :] = unfold(pieces[2 * h * n + group], pieces[(2 * h + 1) * n + group])
     m_high, m_low = halves(mixed[...].T)
-    for copy in copies:
-        copy.wait()
+    projected = []
     for group in range(n):
         at = slice(group * feats, (group + 1) * feats)
-        w_high[at], w_low[at] = halves(whole[at])
-    projected = mm_nt(m_high, w_high[...]) + mm_nt(m_low, w_high[...]) + mm_nt(m_high, w_low[...])
+        copies[group].wait()
+        high, low = halves(whole[at])
+        w_high[at], w_low[at] = high, low
+        projected.append(mm_nt(m_high, high) + mm_nt(m_low, high) + mm_nt(m_high, low))
+    copies[n].wait()
+    projected = jnp.concatenate(projected, axis=1)
     summed = rows[...].reshape(2 * quarter, width) + projected
     mean = jnp.sum(summed, axis=-1, keepdims=True) / width
     second = jnp.sum(summed * summed, axis=-1, keepdims=True) / width
@@ -567,7 +575,7 @@
             pltpu.VMEM((width, width), BF16),
             pltpu.VMEM((2, quarter, width), F32),
             pltpu.VMEM((width, width), F32),
-            pltpu.SemaphoreType.DMA((2,)),
+            pltpu.SemaphoreType.DMA((n + 1,)),
         ],
         1, z_ref, whole_out, rows, *upstream, folded, parked=(1, 2),
     )

time: 210 us -> 211 us (level)
  no operation moved by 1% of the time
where the time goes in v1:
time: 211 us; the launch traced here: 209 us
  waiting for transfers between devices  64.6 us (31%)
  blocking collectives  51.3 us (24%)
  Pallas kernels  41.5 us (20%)
  starting transfers between devices  30.3 us (14%)
  between operations  13.7 us (6%)
  local copies, waits for them, and re-layouts  4.97 us (2%)
  other arithmetic  3.19 us (2%)
    pallas_call x8, Pallas kernels, call(): pl.pallas_call(kernel, out_shape=outs, grid=grid, in_specs=in_specs, out_...  41.5 us
    ppermute x6, waiting for transfers between devices, shift(): return lax.ppermute(x, 'head', [(i, i + by) for i in range(low, high + 1)])  28.8 us
    all_to_all x1, blocking collectives, shards(): grad = lax.all_to_all(grad, ('ctx', 'head'), 0, 0, tiled=True)  18.4 us
    all_to_all x1, blocking collectives, shards(): folded = lax.all_to_all(folded, ('ctx', 'head'), 0, 0, tiled=True)  17 us
    ppermute x9, waiting for transfers between devices, rotate(): return lax.ppermute(x, 'head', [(i, (i + by) % size) for i in range(size)])  16.5 us
    all_to_all x1, blocking collectives, shards(): grad_qkv = [lax.all_to_all(g, 'ctx', 0, 0, tiled=True) for g in grad_qkv]  15.9 us
    all_to_all x1, waiting for transfers between devices, shards(): qkv = lax.all_to_all(qkv, 'ctx', 0, 0, tiled=True)  13.7 us
    ppermute x6, starting transfers between devices, shift(): return lax.ppermute(x, 'head', [(i, i + by) for i in range(low, high + 1)])  12.4 us
  transfers between devices with their start and end apart: 18, of which 10 were waited for; matrix products, arithmetic and copies ran while one was open for 0% of the time, Pallas kernels for 12%

profile of v1, /device:TPU:0, one launch (start us, length us, event | category | flops | bytes accessed | tf_op | source)
XLA Modules:
  0.0 209.5 jit_solution(7209443441873158373)
XLA Ops:
  8.9 1.3 collective-permute-start.1
  10.2 6.4 %collective-permute-start = (f32[512,256]{1,0:T(8,128)S(1)}, f32[512,256]{1,0:T(8,128)}, u32[]{:S(2)}, u32[]{:S(2)}) collective-permute-start(f32[512,256]{1,0:T(8,128)S(1)} %pad_maximum_fusion.own), channel_id=1, source_target_pairs={{0,1},{1,2},{2,3},{4,5},{5,6},{6,7},{8,9},{9,10},{10,11},{12,13},{... | collective-permute-start | bytes 1572872 | tf_op jit(solution)/shard_map/ppermute | solution.py:203
  17.8 2.2 %shard_map.100 = (bf16[768,1024]{1,0:T(8,128)(2,1)}, bf16[768,1024]{1,0:T(8,128)(2,1)}) custom-call(f32[256,1024]{1,0:T(8,128)S(1)} %copy-done.5, f32[256,1024]{1,0:T(8,128)S(1)} %copy-done.6, f32[256,1024]{1,0:T(8,128)S(1)} %copy-done.7), custom_call_target="tpu_custom_call" | custom-call | tf_op jit(solution)/shard_map/pallas_call | solution.py:181
  20.0 5.8 %collective-permute-done.1.d1 = f32[512,256]{1,0:T(8,128)S(1)} collective-permute-done((f32[512,256]{1,0:T(8,128)S(1)}, f32[512,256]{1,0:T(8,128)S(1)}, u32[]{:S(2)}, u32[]{:S(2)}) %collective-permute-start.1) | collective-permute-done | bytes 524320 | tf_op jit(solution)/shard_map/ppermute | solution.py:203
  27.7 1.3 collective-permute-start.3
  29.7 15.9 %collective-permute-done.3.d2 = f32[512,256]{1,0:T(8,128)S(1)} collective-permute-done((f32[512,256]{1,0:T(8,128)S(1)}, f32[512,256]{1,0:T(8,128)S(1)}, u32[]{:S(2)}, u32[]{:S(2)}) %collective-permute-start.3) | collective-permute-done | bytes 524320 | tf_op jit(solution)/shard_map/ppermute | solution.py:203
  45.6 1.5 collective-permute-start.4
  48.5 1.4 copy-done.1
  49.9 1.4 copy-done.2
  51.3 5.2 %shard_map.101 = (f32[8,192,256]{2,1,0:T(8,128)S(1)}, f32[2,64,1024]{2,1,0:T(8,128)S(1)}) custom-call(s32[1]{0:T(128)} %bitcast.z_ref, bf16[768,1024]{1,0:T(8,128)(2,1)S(1)} %copy-done.1, bf16[768,1024]{1,0:T(8,128)(2,1)S(1)} %copy-done.2, f32[512,256]{1,0:T(8,128)S(1)} %pad_maximum_fusion.own, f32[512,256]{1,0:T(8,128)} %collective-permute-done.u1, ...), custom_call_target="tpu_custom_call" | custom-call | tf_op jit(solution)/shard_map/pallas_call | solution.py:181
  56.5 5.9 %collective-permute-done.5.d3 = f32[512,256]{1,0:T(8,128)} collective-permute-done((f32[512,256]{1,0:T(8,128)S(1)}, f32[512,256]{1,0:T(8,128)}, u32[]{:S(2)}, u32[]{:S(2)}) %collective-permute-start.5) | collective-permute-done | bytes 524320 | tf_op jit(solution)/shard_map/ppermute | solution.py:203
  62.5 4.3 %shard_map.102 = (f32[8,200,256]{2,1,0:T(8,128)}, f32[2,64,1024]{2,1,0:T(8,128)}) custom-call(s32[1]{0:T(128)} %bitcast.z_ref, bf16[768,1024]{1,0:T(8,128)(2,1)S(1)} %copy-done.1, bf16[768,1024]{1,0:T(8,128)(2,1)S(1)} %copy-done.2, f32[8,256]{1,0:T(8,128)S(1)} %pad.4.listed, f32[512,256]{1,0:T(8,128)} %collective-permute-done.4.u3, ...), custom_call_target="tpu_custom_call" | custom-call | tf_op jit(solution)/shard_map/pallas_call | solution.py:181
  66.8 4.0 %all-to-all-start = ((f32[8,200,256]{2,1,0:T(8,128)}), f32[8,200,256]{2,1,0:T(8,128)S(1)}, u32[]{:S(2)}, u32[]{:S(2)}) async-start(f32[8,200,256]{2,1,0:T(8,128)} %get-tuple-element.54), calls=%async_computation | async-start | bytes 3276800 | tf_op jit(solution)/shard_map/all_to_all | solution.py:537
  73.0 3.2 %collective-permute-done.8.u3 = f32[64,256]{1,0:T(8,128)S(1)} collective-permute-done((f32[64,256]{1,0:T(8,128)S(1)}, f32[64,256]{1,0:T(8,128)S(1)}, u32[]{:S(2)}, u32[]{:S(2)}) %collective-permute-start.8) | collective-permute-done | bytes 65568 | tf_op jit(solution)/shard_map/ppermute | solution.py:208
  76.2 5.3 %collective-permute-done.7.u2 = f32[64,256]{1,0:T(8,128)S(1)} collective-permute-done((f32[64,256]{1,0:T(8,128)S(1)}, f32[64,256]{1,0:T(8,128)S(1)}, u32[]{:S(2)}, u32[]{:S(2)}) %collective-permute-start.7) | collective-permute-done | bytes 65568 | tf_op jit(solution)/shard_map/ppermute | solution.py:208
  81.5 13.7 %all-to-all-done.qkv = f32[8,200,256]{2,1,0:T(8,128)S(1)} async-done(((f32[8,200,256]{2,1,0:T(8,128)}), f32[8,200,256]{2,1,0:T(8,128)S(1)}, u32[]{:S(2)}, u32[]{:S(2)}) %all-to-all-start) | async-done | bytes 1638432 | tf_op jit(solution)/shard_map/all_to_all | solution.py:537
  95.3 7.4 %shard_map.103 = (f32[16,64,128]{2,1,0:T(8,128)}, f32[32,32,128]{2,1,0:T(8,128)}, bf16[16,640,128]{2,1,0:T(8,128)(2,1)}, bf16[16,640,128]{2,1,0:T(8,128)(2,1)}) custom-call(s32[16,5]{1,0:T(8,128)S(1)} %convert_element_type.29.lists, f32[16,128]{1,0:T(8,128)S(1)} %convert_bitcast_fusion.session_row, f32[8,200,256]{2,1,0:T(8,128)S(1)} %all-to-all-done.qkv), custom_call_target="tpu_custom_call" | custom-call | tf_op jit(solution)/shard_map/pallas_call | solution.py:181
  102.7 17.0 %all_to_all.25.pieces = f32[32,32,128]{2,1,0:T(8,128)S(1)} all-to-all(f32[32,32,128]{2,1,0:T(8,128)} %get-tuple-element.61), channel_id=1, replica_groups=mesh['ctx'=8,'head'=4] {'ctx','head'}, dimensions={0} | all-to-all | bytes 1048576 | tf_op jit(solution)/shard_map/all_to_all | solution.py:567
  119.7 7.1 %shard_map.104 = (f32[32,32,128]{2,1,0:T(8,128)S(1)}, f32[64,1024]{1,0:T(8,128)}) custom-call(s32[1]{0:T(128)} %bitcast.z_ref, f32[1024,1024]{1,0:T(8,128)} %all-gather.2.cloned.1.call-done.parked_whole, f32[2,64,1024]{2,1,0:T(8,128)} %get-tuple-element.52.parked_rows, f32[64,256]{1,0:T(8,128)S(1)} %get-tuple-element.56.u0, ...), custom_call_target="tpu_custom_call" | custom-call | tf_op jit(solution)/shard_map/pallas_call | solution.py:181
  126.8 18.4 %all_to_all.26.grad = f32[32,32,128]{2,1,0:T(8,128)S(1)} all-to-all(f32[32,32,128]{2,1,0:T(8,128)S(1)} %get-tuple-element.65), channel_id=1, replica_groups=mesh['ctx'=8,'head'=4] {'ctx','head'}, dimensions={0} | all-to-all | bytes 1048576 | tf_op jit(solution)/shard_map/all_to_all | solution.py:582
  145.2 9.7 %shard_map.105 = (f32[8,192,128]{2,1,0:T(8,128)}, f32[8,192,128]{2,1,0:T(8,128)S(1)}) custom-call(s32[16,5]{1,0:T(8,128)S(1)} %convert_element_type.29.lists, f32[8,200,256]{2,1,0:T(8,128)S(1)} %all-to-all-done.qkv, bf16[16,640,128]{2,1,0:T(8,128)(2,1)S(1)} %copy-done.3, bf16[16,640,128]{2,1,0:T(8,128)(2,1)S(1)} %copy-done.4, ...), custom_call_target="tpu_custom_call" | custom-call | tf_op jit(solution)/shard_map/pallas_call | solution.py:181
  154.9 15.9 %all_to_all.27.grads = f32[8,192,128]{2,1,0:T(8,128)S(1)} all-to-all(f32[8,192,128]{2,1,0:T(8,128)S(1)} %get-tuple-element.72), channel_id=1, replica_groups=mesh['ctx'=8,'head'=4] {'ctx'}, dimensions={0} | all-to-all | bytes 1572864 | tf_op jit(solution)/shard_map/all_to_all | solution.py:594
  170.8 3.5 %all-to-all-start.3 = ((f32[8,192,128]{2,1,0:T(8,128)}), f32[8,192,128]{2,1,0:T(8,128)S(1)}, u32[]{:S(2)}, u32[]{:S(2)}) async-start(f32[8,192,128]{2,1,0:T(8,128)} %get-tuple-element.67), calls=%async_computation.3 | async-start | bytes 1572864 | tf_op jit(solution)/shard_map/all_to_all | solution.py:594
  174.4 2.8 %shard_map.107 = (f32[128,256]{1,0:T(8,128)S(1)}, f32[128,256]{1,0:T(8,128)S(1)}, f32[128,256]{1,0:T(8,128)S(1)}, f32[128,256]{1,0:T(8,128)S(1)}) custom-call(s32[1]{0:T(128)} %bitcast.z_ref, bf16[768,1024]{1,0:T(8,128)(2,1)} %get-tuple-element.43.w_high.parked_high, bf16[768,1024]{1,0:T(8,128)(2,1)} %get-tuple-element.44.w_low.parked_low, ...), custom_call_target="tpu_custom_call" | custom-call | tf_op jit(solution)/shard_map/pallas_call | solution.py:181
  177.2 1.7 collective-permute-start.12
  179.8 1.5 collective-permute-start.14
  181.3 5.6 %all-to-all-done.3.grads = f32[8,192,128]{2,1,0:T(8,128)S(1)} async-done(((f32[8,192,128]{2,1,0:T(8,128)}), f32[8,192,128]{2,1,0:T(8,128)S(1)}, u32[]{:S(2)}, u32[]{:S(2)}) %all-to-all-start.3) | async-done | bytes 786464 | tf_op jit(solution)/shard_map/all_to_all | solution.py:594
  186.9 2.8 %shard_map.106 = (f32[128,256]{1,0:T(8,128)S(1)}, f32[128,256]{1,0:T(8,128)S(1)}, f32[128,256]{1,0:T(8,128)S(1)}, f32[128,256]{1,0:T(8,128)S(1)}) custom-call(s32[1]{0:T(128)} %bitcast.z_ref, bf16[768,1024]{1,0:T(8,128)(2,1)} %get-tuple-element.43.w_high.parked_high, bf16[768,1024]{1,0:T(8,128)(2,1)} %get-tuple-element.44.w_low.parked_low, ...), custom_call_target="tpu_custom_call" | custom-call | tf_op jit(solution)/shard_map/pallas_call | solution.py:181
  189.7 1.7 collective-permute-start.9
  192.3 1.5 collective-permute-start.11
  193.9 3.1 %collective-permute-done.9 = f32[128,256]{1,0:T(8,128)S(1)} collective-permute-done((f32[128,256]{1,0:T(8,128)S(1)}, f32[128,256]{1,0:T(8,128)S(1)}, u32[]{:S(2)}, u32[]{:S(2)}) %collective-permute-start.9) | collective-permute-done | bytes 131104 | tf_op jit(solution)/shard_map/ppermute | solution.py:208
  197.0 4.9 %collective-permute-done.10 = f32[128,256]{1,0:T(8,128)S(1)} collective-permute-done((f32[128,256]{1,0:T(8,128)S(1)}, f32[128,256]{1,0:T(8,128)S(1)}, u32[]{:S(2)}, u32[]{:S(2)}) %collective-permute-start.10) | collective-permute-done | bytes 131104 | tf_op jit(solution)/shard_map/ppermute | solution.py:208
  (61 shorter events, 12.5 us)
Async XLA Ops:
  6.5 22.4 %copy-start = (f32[256,1024]{1,0:T(8,128)S(1)}, f32[256,1024]{1,0:T(8,128)}, u32[]{:S(2)}) copy-start(f32[256,1024]{1,0:T(8,128)} %param.15) | copy-start | bytes 3145732
  6.5 10.1 %copy-start.5 = (f32[256,1024]{1,0:T(8,128)S(1)}, f32[256,1024]{1,0:T(8,128)}, u32[]{:S(2)}) copy-start(f32[256,1024]{1,0:T(8,128)} %w_query.1) | copy-start | bytes 3145732
  6.5 113.1 %all-gather.2.cloned.1.call-start = ((), (), s32[]{:S(2)}) async-start(), calls=%async_computation.5 | async-start | bytes 4325376 | tf_op jit(solution)/shard_map/all_gather | solution.py:517
  6.5 10.1 %copy-start.6 = (f32[256,1024]{1,0:T(8,128)S(1)}, f32[256,1024]{1,0:T(8,128)}, u32[]{:S(2)}) copy-start(f32[256,1024]{1,0:T(8,128)} %w_key.1) | copy-start | bytes 3145732
  8.9 39.5 %copy-start.14 = (s32[2,5]{1,0:T(2,128)S(1)}, s32[2,5]{1,0:T(2,128)}, u32[]{:S(2)}) copy-start(s32[2,5]{1,0:T(2,128)} %param.19) | copy-start | bytes 124
  8.9 16.8 %collective-permute-start.1 = (f32[512,256]{1,0:T(8,128)S(1)}, f32[512,256]{1,0:T(8,128)S(1)}, u32[]{:S(2)}, u32[]{:S(2)}) collective-permute-start(f32[512,256]{1,0:T(8,128)S(1)} %pad_maximum_fusion.own), channel_id=1, source_target_pairs={{1,0},{2,1},{3,2},{5,4},{6,5},{7,6},{9,8},{10,9},{11,10},{13,12},{... | collective-permute-start | bytes 1572872 | tf_op jit(solution)/shard_map/ppermute | solution.py:203
  10.2 16.7 %collective-permute-start = (f32[512,256]{1,0:T(8,128)S(1)}, f32[512,256]{1,0:T(8,128)}, u32[]{:S(2)}, u32[]{:S(2)}) collective-permute-start(f32[512,256]{1,0:T(8,128)S(1)} %pad_maximum_fusion.own), channel_id=1, source_target_pairs={{0,1},{1,2},{2,3},{4,5},{5,6},{6,7},{8,9},{9,10},{10,11},{12,13},{... | collective-permute-start | bytes 1572872 | tf_op jit(solution)/shard_map/ppermute | solution.py:203
  16.6 1.2 copy-start.7
  27.0 2.7 %collective-permute-start.2 = (f32[512,256]{1,0:T(8,128)}, f32[512,256]{1,0:T(8,128)S(1)}, u32[]{:S(2)}, u32[]{:S(2)}) collective-permute-start(f32[512,256]{1,0:T(8,128)} %collective-permute-done.u1), channel_id=1, source_target_pairs={{1,2},{2,3},{5,6},{6,7},{9,10},{10,11},{13,14},{14,15},{17,18},{18... | collective-permute-start | bytes 1572872 | tf_op jit(solution)/shard_map/ppermute | solution.py:203
  27.7 17.9 %collective-permute-start.3 = (f32[512,256]{1,0:T(8,128)S(1)}, f32[512,256]{1,0:T(8,128)S(1)}, u32[]{:S(2)}, u32[]{:S(2)}) collective-permute-start(f32[512,256]{1,0:T(8,128)S(1)} %collective-permute-done.1.d1), channel_id=1, source_target_pairs={{1,0},{2,1},{5,4},{6,5},{9,8},{10,9},{13,12},{14,13},{17,16},{18,1... | collective-permute-start | bytes 1572872 | tf_op jit(solution)/shard_map/ppermute | solution.py:203
  45.6 10.9 %collective-permute-start.4 = (f32[512,256]{1,0:T(8,128)S(1)}, f32[512,256]{1,0:T(8,128)}, u32[]{:S(2)}, u32[]{:S(2)}) collective-permute-start(f32[512,256]{1,0:T(8,128)S(1)} %collective-permute-done.2.u2), channel_id=1, source_target_pairs={{2,3},{6,7},{10,11},{14,15},{18,19},{22,23},{26,27},{30,31}} | collective-permute-start | bytes 1572872 | tf_op jit(solution)/shard_map/ppermute | solution.py:203
  47.1 15.4 %collective-permute-start.5 = (f32[512,256]{1,0:T(8,128)S(1)}, f32[512,256]{1,0:T(8,128)}, u32[]{:S(2)}, u32[]{:S(2)}) collective-permute-start(f32[512,256]{1,0:T(8,128)S(1)} %collective-permute-done.3.d2), channel_id=1, source_target_pairs={{1,0},{5,4},{9,8},{13,12},{17,16},{21,20},{25,24},{29,28}} | collective-permute-start | bytes 1572872 | tf_op jit(solution)/shard_map/ppermute | solution.py:203
  48.5 1.4 copy-start.1
  49.9 1.4 copy-start.2
  66.7 4.1 %copy-start.11 = (f32[256,256]{1,0:T(8,128)S(1)}, f32[256,256]{1,0:T(8,128)}, u32[]{:S(2)}) copy-start(f32[256,256]{1,0:T(8,128)} %param.17) | copy-start | bytes 786436
  66.7 4.1 %copy-start.13 = (f32[256]{0:T(256)S(1)}, f32[256]{0:T(256)}, u32[]{:S(2)}) copy-start(f32[256]{0:T(256)} %param.16) | copy-start | bytes 3076
  66.8 6.2 %copy-start.12 = (s32[2048]{0:T(1024)S(1)}, s32[2048]{0:T(1024)}, u32[]{:S(2)}) copy-start(s32[2048]{0:T(1024)} %param.18) | copy-start | bytes 24580
  66.8 28.4 %all-to-all-start = ((f32[8,200,256]{2,1,0:T(8,128)}), f32[8,200,256]{2,1,0:T(8,128)S(1)}, u32[]{:S(2)}, u32[]{:S(2)}) async-start(f32[8,200,256]{2,1,0:T(8,128)} %get-tuple-element.54), calls=%async_computation | async-start | bytes 3276800 | tf_op jit(solution)/shard_map/all_to_all | solution.py:537
  70.9 5.3 %collective-permute-start.8 = (f32[64,256]{1,0:T(8,128)S(1)}, f32[64,256]{1,0:T(8,128)S(1)}, u32[]{:S(2)}, u32[]{:S(2)}) collective-permute-start(f32[64,256]{1,0:T(8,128)S(1)} %get-tuple-element.79), channel_id=1, source_target_pairs={{0,3},{1,0},{2,1},{3,2},{4,7},{5,4},{6,5},{7,6},{8,11},{9,8},{10,9... | collective-permute-start | bytes 196616 | tf_op jit(solution)/shard_map/ppermute | solution.py:208
  71.0 10.6 %collective-permute-start.7 = (f32[64,256]{1,0:T(8,128)S(1)}, f32[64,256]{1,0:T(8,128)S(1)}, u32[]{:S(2)}, u32[]{:S(2)}) collective-permute-start(f32[64,256]{1,0:T(8,128)S(1)} %get-tuple-element.80), channel_id=1, source_target_pairs={{0,2},{1,3},{2,0},{3,1},{4,6},{5,7},{6,4},{7,5},{8,10},{9,11},{10,... | collective-permute-start | bytes 196616 | tf_op jit(solution)/shard_map/ppermute | solution.py:208
  71.8 9.7 %collective-permute-start.6 = (f32[64,256]{1,0:T(8,128)S(1)}, f32[64,256]{1,0:T(8,128)S(1)}, u32[]{:S(2)}, u32[]{:S(2)}) collective-permute-start(f32[64,256]{1,0:T(8,128)S(1)} %get-tuple-element.81), channel_id=1, source_target_pairs={{0,1},{1,2},{2,3},{3,0},{4,5},{5,6},{6,7},{7,4},{8,9},{9,10},{10,1... | collective-permute-start | bytes 196616 | tf_op jit(solution)/shard_map/ppermute | solution.py:208
  119.7 25.5 %copy-start.3 = (bf16[16,640,128]{2,1,0:T(8,128)(2,1)S(1)}, bf16[16,640,128]{2,1,0:T(8,128)(2,1)}, u32[]{:S(2)}) copy-start(bf16[16,640,128]{2,1,0:T(8,128)(2,1)} %get-tuple-element.63.p_high) | copy-start | bytes 7864324
  119.7 25.5 %copy-start.4 = (bf16[16,640,128]{2,1,0:T(8,128)(2,1)S(1)}, bf16[16,640,128]{2,1,0:T(8,128)(2,1)}, u32[]{:S(2)}) copy-start(bf16[16,640,128]{2,1,0:T(8,128)(2,1)} %get-tuple-element.64.p_low) | copy-start | bytes 7864324
  119.7 25.5 %copy-start.8 = (f32[16,64,128]{2,1,0:T(8,128)S(1)}, f32[16,64,128]{2,1,0:T(8,128)}, u32[]{:S(2)}) copy-start(f32[16,64,128]{2,1,0:T(8,128)} %get-tuple-element.66.mixed) | copy-start | bytes 1572868
  170.8 16.1 %all-to-all-start.3 = ((f32[8,192,128]{2,1,0:T(8,128)}), f32[8,192,128]{2,1,0:T(8,128)S(1)}, u32[]{:S(2)}, u32[]{:S(2)}) async-start(f32[8,192,128]{2,1,0:T(8,128)} %get-tuple-element.67), calls=%async_computation.3 | async-start | bytes 1572864 | tf_op jit(solution)/shard_map/all_to_all | solution.py:594
  177.2 15.2 %collective-permute-start.12 = (f32[128,256]{1,0:T(8,128)S(1)}, f32[128,256]{1,0:T(8,128)S(1)}, u32[]{:S(2)}, u32[]{:S(2)}) collective-permute-start(f32[128,256]{1,0:T(8,128)S(1)} %get-tuple-element.74), channel_id=1, source_target_pairs={{0,1},{1,2},{2,3},{3,0},{4,5},{5,6},{6,7},{7,4},{8,9},{9,10},{10,1... | collective-permute-start | bytes 393224 | tf_op jit(solution)/shard_map/ppermute | solution.py:208
  178.9 15.0 %collective-permute-start.13 = (f32[128,256]{1,0:T(8,128)S(1)}, f32[128,256]{1,0:T(8,128)S(1)}, u32[]{:S(2)}, u32[]{:S(2)}) collective-permute-start(f32[128,256]{1,0:T(8,128)S(1)} %get-tuple-element.75), channel_id=1, source_target_pairs={{0,2},{1,3},{2,0},{3,1},{4,6},{5,7},{6,4},{7,5},{8,10},{9,11},{10,... | collective-permute-start | bytes 393224 | tf_op jit(solution)/shard_map/ppermute | solution.py:208
  179.8 22.1 %copy-start.10 = (f32[256,256]{1,0:T(8,128)S(1)}, f32[256,256]{1,0:T(8,128)}, u32[]{:S(2)}) copy-start(f32[256,256]{1,0:T(8,128)} %copy-done.9) | copy-start | bytes 786436
  179.8 14.0 %collective-permute-start.14 = (f32[128,256]{1,0:T(8,128)S(1)}, f32[128,256]{1,0:T(8,128)S(1)}, u32[]{:S(2)}, u32[]{:S(2)}) collective-permute-start(f32[128,256]{1,0:T(8,128)S(1)} %get-tuple-element.76), channel_id=1, source_target_pairs={{0,3},{1,0},{2,1},{3,2},{4,7},{5,4},{6,5},{7,6},{8,11},{9,8},{10,9... | collective-permute-start | bytes 393224 | tf_op jit(solution)/shard_map/ppermute | solution.py:208
  189.7 7.3 %collective-permute-start.9 = (f32[128,256]{1,0:T(8,128)S(1)}, f32[128,256]{1,0:T(8,128)S(1)}, u32[]{:S(2)}, u32[]{:S(2)}) collective-permute-start(f32[128,256]{1,0:T(8,128)S(1)} %get-tuple-element.69), channel_id=1, source_target_pairs={{0,1},{1,2},{2,3},{3,0},{4,5},{5,6},{6,7},{7,4},{8,9},{9,10},{10,1... | collective-permute-start | bytes 393224 | tf_op jit(solution)/shard_map/ppermute | solution.py:208
  191.4 10.4 %collective-permute-start.10 = (f32[128,256]{1,0:T(8,128)S(1)}, f32[128,256]{1,0:T(8,128)S(1)}, u32[]{:S(2)}, u32[]{:S(2)}) collective-permute-start(f32[128,256]{1,0:T(8,128)S(1)} %get-tuple-element.70), channel_id=1, source_target_pairs={{0,2},{1,3},{2,0},{3,1},{4,6},{5,7},{6,4},{7,5},{8,10},{9,11},{10,... | collective-permute-start | bytes 393224 | tf_op jit(solution)/shard_map/ppermute | solution.py:208
  192.3 9.5 %collective-permute-start.11 = (f32[128,256]{1,0:T(8,128)S(1)}, f32[128,256]{1,0:T(8,128)S(1)}, u32[]{:S(2)}, u32[]{:S(2)}) collective-permute-start(f32[128,256]{1,0:T(8,128)S(1)} %get-tuple-element.71), channel_id=1, source_target_pairs={{0,3},{1,0},{2,1},{3,2},{4,7},{5,4},{6,5},{7,6},{8,11},{9,8},{10,9... | collective-permute-start | bytes 393224 | tf_op jit(solution)/shard_map/ppermute | solution.py:208
  (1 other events, 1.1 us)
Sparse Core Ops, SparseCore 0:
  45.7 64.3 all-gather.1

commit v2 on v0

--- a/solution.py
+++ b/solution.py
@@ -461,7 +461,7 @@
 
 HD = 64
 NBLOCKS = 16
-GROUP = 4
+GROUP = 8
 SCALE = 1.0 / math.sqrt(HD)
 
 

time: 210 us -> 209 us (level)
  no operation moved by 1% of the time
where the time goes in v2:
time: 209 us; the launch traced here: 208 us
  waiting for transfers between devices  64.6 us (31%)
  blocking collectives  51.5 us (25%)
  Pallas kernels  39.9 us (19%)
  starting transfers between devices  30.3 us (14%)
  between operations  13.7 us (7%)
  local copies, waits for them, and re-layouts  4.97 us (2%)
  other arithmetic  3.19 us (2%)
    pallas_call x8, Pallas kernels, call(): pl.pallas_call(kernel, out_shape=outs, grid=grid, in_specs=in_specs, out_...  39.9 us
    ppermute x6, waiting for transfers between devices, shift(): return lax.ppermute(x, 'head', [(i, i + by) for i in range(low, high + 1)])  28.8 us
    all_to_all x1, blocking collectives, shards(): grad = lax.all_to_all(grad, ('ctx', 'head'), 0, 0, tiled=True)  18.5 us
    all_to_all x1, blocking collectives, shards(): folded = lax.all_to_all(folded, ('ctx', 'head'), 0, 0, tiled=True)  17.1 us
    ppermute x9, waiting for transfers between devices, rotate(): return lax.ppermute(x, 'head', [(i, (i + by) % size) for i in range(size)])  16.5 us
    all_to_all x1, blocking collectives, shards(): grad_qkv = [lax.all_to_all(g, 'ctx', 0, 0, tiled=True) for g in grad_qkv]  15.9 us
    all_to_all x1, waiting for transfers between devices, shards(): qkv = lax.all_to_all(qkv, 'ctx', 0, 0, tiled=True)  13.7 us
    ppermute x6, starting transfers between devices, shift(): return lax.ppermute(x, 'head', [(i, i + by) for i in range(low, high + 1)])  12.4 us
  transfers between devices with their start and end apart: 18, of which 10 were waited for; matrix products, arithmetic and copies ran while one was open for 0% of the time, Pallas kernels for 12%

profile of v2, /device:TPU:0, one launch (start us, length us, event | category | flops | bytes accessed | tf_op | source)
XLA Modules:
  0.0 208.1 jit_solution(1036549257944562511)
XLA Ops:
  8.9 1.3 collective-permute-start.1
  10.2 6.4 %collective-permute-start = (f32[512,256]{1,0:T(8,128)S(1)}, f32[512,256]{1,0:T(8,128)}, u32[]{:S(2)}, u32[]{:S(2)}) collective-permute-start(f32[512,256]{1,0:T(8,128)S(1)} %pad_maximum_fusion.own), channel_id=1, source_target_pairs={{0,1},{1,2},{2,3},{4,5},{5,6},{6,7},{8,9},{9,10},{10,11},{12,13},{... | collective-permute-start | bytes 1572872 | tf_op jit(solution)/shard_map/ppermute | solution.py:203
  17.8 2.2 %shard_map.100 = (bf16[768,1024]{1,0:T(8,128)(2,1)}, bf16[768,1024]{1,0:T(8,128)(2,1)}) custom-call(f32[256,1024]{1,0:T(8,128)S(1)} %copy-done.5, f32[256,1024]{1,0:T(8,128)S(1)} %copy-done.6, f32[256,1024]{1,0:T(8,128)S(1)} %copy-done.7), custom_call_target="tpu_custom_call" | custom-call | tf_op jit(solution)/shard_map/pallas_call | solution.py:181
  20.0 5.8 %collective-permute-done.1.d1 = f32[512,256]{1,0:T(8,128)S(1)} collective-permute-done((f32[512,256]{1,0:T(8,128)S(1)}, f32[512,256]{1,0:T(8,128)S(1)}, u32[]{:S(2)}, u32[]{:S(2)}) %collective-permute-start.1) | collective-permute-done | bytes 524320 | tf_op jit(solution)/shard_map/ppermute | solution.py:203
  27.7 1.3 collective-permute-start.3
  29.7 15.9 %collective-permute-done.3.d2 = f32[512,256]{1,0:T(8,128)S(1)} collective-permute-done((f32[512,256]{1,0:T(8,128)S(1)}, f32[512,256]{1,0:T(8,128)S(1)}, u32[]{:S(2)}, u32[]{:S(2)}) %collective-permute-start.3) | collective-permute-done | bytes 524320 | tf_op jit(solution)/shard_map/ppermute | solution.py:203
  45.6 1.5 collective-permute-start.4
  48.5 1.4 copy-done.1
  49.9 1.4 copy-done.2
  51.3 5.2 %shard_map.101 = (f32[8,192,256]{2,1,0:T(8,128)S(1)}, f32[2,64,1024]{2,1,0:T(8,128)S(1)}) custom-call(s32[1]{0:T(128)} %bitcast.z_ref, bf16[768,1024]{1,0:T(8,128)(2,1)S(1)} %copy-done.1, bf16[768,1024]{1,0:T(8,128)(2,1)S(1)} %copy-done.2, f32[512,256]{1,0:T(8,128)S(1)} %pad_maximum_fusion.own, f32[512,256]{1,0:T(8,128)} %collective-permute-done.u1, ...), custom_call_target="tpu_custom_call" | custom-call | tf_op jit(solution)/shard_map/pallas_call | solution.py:181
  56.5 5.9 %collective-permute-done.5.d3 = f32[512,256]{1,0:T(8,128)} collective-permute-done((f32[512,256]{1,0:T(8,128)S(1)}, f32[512,256]{1,0:T(8,128)}, u32[]{:S(2)}, u32[]{:S(2)}) %collective-permute-start.5) | collective-permute-done | bytes 524320 | tf_op jit(solution)/shard_map/ppermute | solution.py:203
  62.5 4.3 %shard_map.102 = (f32[8,200,256]{2,1,0:T(8,128)}, f32[2,64,1024]{2,1,0:T(8,128)}) custom-call(s32[1]{0:T(128)} %bitcast.z_ref, bf16[768,1024]{1,0:T(8,128)(2,1)S(1)} %copy-done.1, bf16[768,1024]{1,0:T(8,128)(2,1)S(1)} %copy-done.2, f32[8,256]{1,0:T(8,128)S(1)} %pad.4.listed, f32[512,256]{1,0:T(8,128)} %collective-permute-done.4.u3, ...), custom_call_target="tpu_custom_call" | custom-call | tf_op jit(solution)/shard_map/pallas_call | solution.py:181
  66.8 4.0 %all-to-all-start = ((f32[8,200,256]{2,1,0:T(8,128)}), f32[8,200,256]{2,1,0:T(8,128)S(1)}, u32[]{:S(2)}, u32[]{:S(2)}) async-start(f32[8,200,256]{2,1,0:T(8,128)} %get-tuple-element.54), calls=%async_computation | async-start | bytes 3276800 | tf_op jit(solution)/shard_map/all_to_all | solution.py:529
  73.0 3.2 %collective-permute-done.8.u3 = f32[64,256]{1,0:T(8,128)S(1)} collective-permute-done((f32[64,256]{1,0:T(8,128)S(1)}, f32[64,256]{1,0:T(8,128)S(1)}, u32[]{:S(2)}, u32[]{:S(2)}) %collective-permute-start.8) | collective-permute-done | bytes 65568 | tf_op jit(solution)/shard_map/ppermute | solution.py:208
  76.2 5.3 %collective-permute-done.7.u2 = f32[64,256]{1,0:T(8,128)S(1)} collective-permute-done((f32[64,256]{1,0:T(8,128)S(1)}, f32[64,256]{1,0:T(8,128)S(1)}, u32[]{:S(2)}, u32[]{:S(2)}) %collective-permute-start.7) | collective-permute-done | bytes 65568 | tf_op jit(solution)/shard_map/ppermute | solution.py:208
  81.5 13.7 %all-to-all-done.qkv = f32[8,200,256]{2,1,0:T(8,128)S(1)} async-done(((f32[8,200,256]{2,1,0:T(8,128)}), f32[8,200,256]{2,1,0:T(8,128)S(1)}, u32[]{:S(2)}, u32[]{:S(2)}) %all-to-all-start) | async-done | bytes 1638432 | tf_op jit(solution)/shard_map/all_to_all | solution.py:529
  95.3 7.1 %shard_map.103 = (f32[16,64,128]{2,1,0:T(8,128)}, f32[32,32,128]{2,1,0:T(8,128)}, bf16[16,640,128]{2,1,0:T(8,128)(2,1)}, bf16[16,640,128]{2,1,0:T(8,128)(2,1)}) custom-call(s32[16,5]{1,0:T(8,128)S(1)} %convert_element_type.29.lists, f32[16,128]{1,0:T(8,128)S(1)} %convert_bitcast_fusion.session_row, f32[8,200,256]{2,1,0:T(8,128)S(1)} %all-to-all-done.qkv), custom_call_target="tpu_custom_call" | custom-call | tf_op jit(solution)/shard_map/pallas_call | solution.py:181
  102.4 17.1 %all_to_all.25.pieces = f32[32,32,128]{2,1,0:T(8,128)S(1)} all-to-all(f32[32,32,128]{2,1,0:T(8,128)} %get-tuple-element.61), channel_id=1, replica_groups=mesh['ctx'=8,'head'=4] {'ctx','head'}, dimensions={0} | all-to-all | bytes 1048576 | tf_op jit(solution)/shard_map/all_to_all | solution.py:559
  119.5 6.4 %shard_map.104 = (f32[32,32,128]{2,1,0:T(8,128)S(1)}, f32[64,1024]{1,0:T(8,128)}) custom-call(s32[1]{0:T(128)} %bitcast.z_ref, f32[1024,1024]{1,0:T(8,128)} %all-gather.2.cloned.1.call-done.parked_whole, f32[2,64,1024]{2,1,0:T(8,128)} %get-tuple-element.52.parked_rows, f32[64,256]{1,0:T(8,128)S(1)} %get-tuple-element.56.u0, ...), custom_call_target="tpu_custom_call" | custom-call | tf_op jit(solution)/shard_map/pallas_call | solution.py:181
  125.9 18.5 %all_to_all.26.grad = f32[32,32,128]{2,1,0:T(8,128)S(1)} all-to-all(f32[32,32,128]{2,1,0:T(8,128)S(1)} %get-tuple-element.65), channel_id=1, replica_groups=mesh['ctx'=8,'head'=4] {'ctx','head'}, dimensions={0} | all-to-all | bytes 1048576 | tf_op jit(solution)/shard_map/all_to_all | solution.py:574
  144.4 9.2 %shard_map.105 = (f32[8,192,128]{2,1,0:T(8,128)}, f32[8,192,128]{2,1,0:T(8,128)S(1)}) custom-call(s32[16,5]{1,0:T(8,128)S(1)} %convert_element_type.29.lists, f32[8,200,256]{2,1,0:T(8,128)S(1)} %all-to-all-done.qkv, bf16[16,640,128]{2,1,0:T(8,128)(2,1)S(1)} %copy-done.3, bf16[16,640,128]{2,1,0:T(8,128)(2,1)S(1)} %copy-done.4, ...), custom_call_target="tpu_custom_call" | custom-call | tf_op jit(solution)/shard_map/pallas_call | solution.py:181
  153.7 15.9 %all_to_all.27.grads = f32[8,192,128]{2,1,0:T(8,128)S(1)} all-to-all(f32[8,192,128]{2,1,0:T(8,128)S(1)} %get-tuple-element.72), channel_id=1, replica_groups=mesh['ctx'=8,'head'=4] {'ctx'}, dimensions={0} | all-to-all | bytes 1572864 | tf_op jit(solution)/shard_map/all_to_all | solution.py:586
  169.6 3.5 %all-to-all-start.3 = ((f32[8,192,128]{2,1,0:T(8,128)}), f32[8,192,128]{2,1,0:T(8,128)S(1)}, u32[]{:S(2)}, u32[]{:S(2)}) async-start(f32[8,192,128]{2,1,0:T(8,128)} %get-tuple-element.67), calls=%async_computation.3 | async-start | bytes 1572864 | tf_op jit(solution)/shard_map/all_to_all | solution.py:586
  173.1 2.8 %shard_map.107 = (f32[128,256]{1,0:T(8,128)S(1)}, f32[128,256]{1,0:T(8,128)S(1)}, f32[128,256]{1,0:T(8,128)S(1)}, f32[128,256]{1,0:T(8,128)S(1)}) custom-call(s32[1]{0:T(128)} %bitcast.z_ref, bf16[768,1024]{1,0:T(8,128)(2,1)} %get-tuple-element.43.w_high.parked_high, bf16[768,1024]{1,0:T(8,128)(2,1)} %get-tuple-element.44.w_low.parked_low, ...), custom_call_target="tpu_custom_call" | custom-call | tf_op jit(solution)/shard_map/pallas_call | solution.py:181
  175.9 1.7 collective-permute-start.12
  178.5 1.5 collective-permute-start.14
  180.0 5.6 %all-to-all-done.3.grads = f32[8,192,128]{2,1,0:T(8,128)S(1)} async-done(((f32[8,192,128]{2,1,0:T(8,128)}), f32[8,192,128]{2,1,0:T(8,128)S(1)}, u32[]{:S(2)}, u32[]{:S(2)}) %all-to-all-start.3) | async-done | bytes 786464 | tf_op jit(solution)/shard_map/all_to_all | solution.py:586
  185.6 2.8 %shard_map.106 = (f32[128,256]{1,0:T(8,128)S(1)}, f32[128,256]{1,0:T(8,128)S(1)}, f32[128,256]{1,0:T(8,128)S(1)}, f32[128,256]{1,0:T(8,128)S(1)}) custom-call(s32[1]{0:T(128)} %bitcast.z_ref, bf16[768,1024]{1,0:T(8,128)(2,1)} %get-tuple-element.43.w_high.parked_high, bf16[768,1024]{1,0:T(8,128)(2,1)} %get-tuple-element.44.w_low.parked_low, ...), custom_call_target="tpu_custom_call" | custom-call | tf_op jit(solution)/shard_map/pallas_call | solution.py:181
  188.4 1.7 collective-permute-start.9
  191.0 1.5 collective-permute-start.11
  192.6 3.1 %collective-permute-done.9 = f32[128,256]{1,0:T(8,128)S(1)} collective-permute-done((f32[128,256]{1,0:T(8,128)S(1)}, f32[128,256]{1,0:T(8,128)S(1)}, u32[]{:S(2)}, u32[]{:S(2)}) %collective-permute-start.9) | collective-permute-done | bytes 131104 | tf_op jit(solution)/shard_map/ppermute | solution.py:208
  195.7 4.8 %collective-permute-done.10 = f32[128,256]{1,0:T(8,128)S(1)} collective-permute-done((f32[128,256]{1,0:T(8,128)S(1)}, f32[128,256]{1,0:T(8,128)S(1)}, u32[]{:S(2)}, u32[]{:S(2)}) %collective-permute-start.10) | collective-permute-done | bytes 131104 | tf_op jit(solution)/shard_map/ppermute | solution.py:208
  (61 shorter events, 12.5 us)
Async XLA Ops:
  6.5 22.4 %copy-start = (f32[256,1024]{1,0:T(8,128)S(1)}, f32[256,1024]{1,0:T(8,128)}, u32[]{:S(2)}) copy-start(f32[256,1024]{1,0:T(8,128)} %param.15) | copy-start | bytes 3145732
  6.5 10.1 %copy-start.5 = (f32[256,1024]{1,0:T(8,128)S(1)}, f32[256,1024]{1,0:T(8,128)}, u32[]{:S(2)}) copy-start(f32[256,1024]{1,0:T(8,128)} %w_query.1) | copy-start | bytes 3145732
  6.5 113.0 %all-gather.2.cloned.1.call-start = ((), (), s32[]{:S(2)}) async-start(), calls=%async_computation.5 | async-start | bytes 4325376 | tf_op jit(solution)/shard_map/all_gather | solution.py:509
  6.5 10.1 %copy-start.6 = (f32[256,1024]{1,0:T(8,128)S(1)}, f32[256,1024]{1,0:T(8,128)}, u32[]{:S(2)}) copy-start(f32[256,1024]{1,0:T(8,128)} %w_key.1) | copy-start | bytes 3145732
  8.9 39.5 %copy-start.14 = (s32[2,5]{1,0:T(2,128)S(1)}, s32[2,5]{1,0:T(2,128)}, u32[]{:S(2)}) copy-start(s32[2,5]{1,0:T(2,128)} %param.19) | copy-start | bytes 124
  8.9 16.8 %collective-permute-start.1 = (f32[512,256]{1,0:T(8,128)S(1)}, f32[512,256]{1,0:T(8,128)S(1)}, u32[]{:S(2)}, u32[]{:S(2)}) collective-permute-start(f32[512,256]{1,0:T(8,128)S(1)} %pad_maximum_fusion.own), channel_id=1, source_target_pairs={{1,0},{2,1},{3,2},{5,4},{6,5},{7,6},{9,8},{10,9},{11,10},{13,12},{... | collective-permute-start | bytes 1572872 | tf_op jit(solution)/shard_map/ppermute | solution.py:203
  10.2 16.7 %collective-permute-start = (f32[512,256]{1,0:T(8,128)S(1)}, f32[512,256]{1,0:T(8,128)}, u32[]{:S(2)}, u32[]{:S(2)}) collective-permute-start(f32[512,256]{1,0:T(8,128)S(1)} %pad_maximum_fusion.own), channel_id=1, source_target_pairs={{0,1},{1,2},{2,3},{4,5},{5,6},{6,7},{8,9},{9,10},{10,11},{12,13},{... | collective-permute-start | bytes 1572872 | tf_op jit(solution)/shard_map/ppermute | solution.py:203
  16.6 1.2 copy-start.7
  27.0 2.7 %collective-permute-start.2 = (f32[512,256]{1,0:T(8,128)}, f32[512,256]{1,0:T(8,128)S(1)}, u32[]{:S(2)}, u32[]{:S(2)}) collective-permute-start(f32[512,256]{1,0:T(8,128)} %collective-permute-done.u1), channel_id=1, source_target_pairs={{1,2},{2,3},{5,6},{6,7},{9,10},{10,11},{13,14},{14,15},{17,18},{18... | collective-permute-start | bytes 1572872 | tf_op jit(solution)/shard_map/ppermute | solution.py:203
  27.7 17.9 %collective-permute-start.3 = (f32[512,256]{1,0:T(8,128)S(1)}, f32[512,256]{1,0:T(8,128)S(1)}, u32[]{:S(2)}, u32[]{:S(2)}) collective-permute-start(f32[512,256]{1,0:T(8,128)S(1)} %collective-permute-done.1.d1), channel_id=1, source_target_pairs={{1,0},{2,1},{5,4},{6,5},{9,8},{10,9},{13,12},{14,13},{17,16},{18,1... | collective-permute-start | bytes 1572872 | tf_op jit(solution)/shard_map/ppermute | solution.py:203
  45.6 10.9 %collective-permute-start.4 = (f32[512,256]{1,0:T(8,128)S(1)}, f32[512,256]{1,0:T(8,128)}, u32[]{:S(2)}, u32[]{:S(2)}) collective-permute-start(f32[512,256]{1,0:T(8,128)S(1)} %collective-permute-done.2.u2), channel_id=1, source_target_pairs={{2,3},{6,7},{10,11},{14,15},{18,19},{22,23},{26,27},{30,31}} | collective-permute-start | bytes 1572872 | tf_op jit(solution)/shard_map/ppermute | solution.py:203
  47.1 15.4 %collective-permute-start.5 = (f32[512,256]{1,0:T(8,128)S(1)}, f32[512,256]{1,0:T(8,128)}, u32[]{:S(2)}, u32[]{:S(2)}) collective-permute-start(f32[512,256]{1,0:T(8,128)S(1)} %collective-permute-done.3.d2), channel_id=1, source_target_pairs={{1,0},{5,4},{9,8},{13,12},{17,16},{21,20},{25,24},{29,28}} | collective-permute-start | bytes 1572872 | tf_op jit(solution)/shard_map/ppermute | solution.py:203
  48.5 1.4 copy-start.1
  49.9 1.4 copy-start.2
  66.7 4.1 %copy-start.11 = (f32[256,256]{1,0:T(8,128)S(1)}, f32[256,256]{1,0:T(8,128)}, u32[]{:S(2)}) copy-start(f32[256,256]{1,0:T(8,128)} %param.17) | copy-start | bytes 786436
  66.7 4.1 %copy-start.13 = (f32[256]{0:T(256)S(1)}, f32[256]{0:T(256)}, u32[]{:S(2)}) copy-start(f32[256]{0:T(256)} %param.16) | copy-start | bytes 3076
  66.8 6.2 %copy-start.12 = (s32[2048]{0:T(1024)S(1)}, s32[2048]{0:T(1024)}, u32[]{:S(2)}) copy-start(s32[2048]{0:T(1024)} %param.18) | copy-start | bytes 24580
  66.8 28.4 %all-to-all-start = ((f32[8,200,256]{2,1,0:T(8,128)}), f32[8,200,256]{2,1,0:T(8,128)S(1)}, u32[]{:S(2)}, u32[]{:S(2)}) async-start(f32[8,200,256]{2,1,0:T(8,128)} %get-tuple-element.54), calls=%async_computation | async-start | bytes 3276800 | tf_op jit(solution)/shard_map/all_to_all | solution.py:529
  70.9 5.3 %collective-permute-start.8 = (f32[64,256]{1,0:T(8,128)S(1)}, f32[64,256]{1,0:T(8,128)S(1)}, u32[]{:S(2)}, u32[]{:S(2)}) collective-permute-start(f32[64,256]{1,0:T(8,128)S(1)} %get-tuple-element.79), channel_id=1, source_target_pairs={{0,3},{1,0},{2,1},{3,2},{4,7},{5,4},{6,5},{7,6},{8,11},{9,8},{10,9... | collective-permute-start | bytes 196616 | tf_op jit(solution)/shard_map/ppermute | solution.py:208
  71.0 10.6 %collective-permute-start.7 = (f32[64,256]{1,0:T(8,128)S(1)}, f32[64,256]{1,0:T(8,128)S(1)}, u32[]{:S(2)}, u32[]{:S(2)}) collective-permute-start(f32[64,256]{1,0:T(8,128)S(1)} %get-tuple-element.80), channel_id=1, source_target_pairs={{0,2},{1,3},{2,0},{3,1},{4,6},{5,7},{6,4},{7,5},{8,10},{9,11},{10,... | collective-permute-start | bytes 196616 | tf_op jit(solution)/shard_map/ppermute | solution.py:208
  71.8 9.7 %collective-permute-start.6 = (f32[64,256]{1,0:T(8,128)S(1)}, f32[64,256]{1,0:T(8,128)S(1)}, u32[]{:S(2)}, u32[]{:S(2)}) collective-permute-start(f32[64,256]{1,0:T(8,128)S(1)} %get-tuple-element.81), channel_id=1, source_target_pairs={{0,1},{1,2},{2,3},{3,0},{4,5},{5,6},{6,7},{7,4},{8,9},{9,10},{10,1... | collective-permute-start | bytes 196616 | tf_op jit(solution)/shard_map/ppermute | solution.py:208
  119.5 24.9 %copy-start.3 = (bf16[16,640,128]{2,1,0:T(8,128)(2,1)S(1)}, bf16[16,640,128]{2,1,0:T(8,128)(2,1)}, u32[]{:S(2)}) copy-start(bf16[16,640,128]{2,1,0:T(8,128)(2,1)} %get-tuple-element.63.p_high) | copy-start | bytes 7864324
  119.5 24.9 %copy-start.4 = (bf16[16,640,128]{2,1,0:T(8,128)(2,1)S(1)}, bf16[16,640,128]{2,1,0:T(8,128)(2,1)}, u32[]{:S(2)}) copy-start(bf16[16,640,128]{2,1,0:T(8,128)(2,1)} %get-tuple-element.64.p_low) | copy-start | bytes 7864324
  119.5 24.9 %copy-start.8 = (f32[16,64,128]{2,1,0:T(8,128)S(1)}, f32[16,64,128]{2,1,0:T(8,128)}, u32[]{:S(2)}) copy-start(f32[16,64,128]{2,1,0:T(8,128)} %get-tuple-element.66.mixed) | copy-start | bytes 1572868
  169.6 16.1 %all-to-all-start.3 = ((f32[8,192,128]{2,1,0:T(8,128)}), f32[8,192,128]{2,1,0:T(8,128)S(1)}, u32[]{:S(2)}, u32[]{:S(2)}) async-start(f32[8,192,128]{2,1,0:T(8,128)} %get-tuple-element.67), calls=%async_computation.3 | async-start | bytes 1572864 | tf_op jit(solution)/shard_map/all_to_all | solution.py:586
  175.9 15.1 %collective-permute-start.12 = (f32[128,256]{1,0:T(8,128)S(1)}, f32[128,256]{1,0:T(8,128)S(1)}, u32[]{:S(2)}, u32[]{:S(2)}) collective-permute-start(f32[128,256]{1,0:T(8,128)S(1)} %get-tuple-element.74), channel_id=1, source_target_pairs={{0,1},{1,2},{2,3},{3,0},{4,5},{5,6},{6,7},{7,4},{8,9},{9,10},{10,1... | collective-permute-start | bytes 393224 | tf_op jit(solution)/shard_map/ppermute | solution.py:208
  177.6 15.0 %collective-permute-start.13 = (f32[128,256]{1,0:T(8,128)S(1)}, f32[128,256]{1,0:T(8,128)S(1)}, u32[]{:S(2)}, u32[]{:S(2)}) collective-permute-start(f32[128,256]{1,0:T(8,128)S(1)} %get-tuple-element.75), channel_id=1, source_target_pairs={{0,2},{1,3},{2,0},{3,1},{4,6},{5,7},{6,4},{7,5},{8,10},{9,11},{10,... | collective-permute-start | bytes 393224 | tf_op jit(solution)/shard_map/ppermute | solution.py:208
  178.5 22.0 %copy-start.10 = (f32[256,256]{1,0:T(8,128)S(1)}, f32[256,256]{1,0:T(8,128)}, u32[]{:S(2)}) copy-start(f32[256,256]{1,0:T(8,128)} %copy-done.9) | copy-start | bytes 786436
  178.5 14.0 %collective-permute-start.14 = (f32[128,256]{1,0:T(8,128)S(1)}, f32[128,256]{1,0:T(8,128)S(1)}, u32[]{:S(2)}, u32[]{:S(2)}) collective-permute-start(f32[128,256]{1,0:T(8,128)S(1)} %get-tuple-element.76), channel_id=1, source_target_pairs={{0,3},{1,0},{2,1},{3,2},{4,7},{5,4},{6,5},{7,6},{8,11},{9,8},{10,9... | collective-permute-start | bytes 393224 | tf_op jit(solution)/shard_map/ppermute | solution.py:208
  188.4 7.3 %collective-permute-start.9 = (f32[128,256]{1,0:T(8,128)S(1)}, f32[128,256]{1,0:T(8,128)S(1)}, u32[]{:S(2)}, u32[]{:S(2)}) collective-permute-start(f32[128,256]{1,0:T(8,128)S(1)} %get-tuple-element.69), channel_id=1, source_target_pairs={{0,1},{1,2},{2,3},{3,0},{4,5},{5,6},{6,7},{7,4},{8,9},{9,10},{10,1... | collective-permute-start | bytes 393224 | tf_op jit(solution)/shard_map/ppermute | solution.py:208
  190.1 10.4 %collective-permute-start.10 = (f32[128,256]{1,0:T(8,128)S(1)}, f32[128,256]{1,0:T(8,128)S(1)}, u32[]{:S(2)}, u32[]{:S(2)}) collective-permute-start(f32[128,256]{1,0:T(8,128)S(1)} %get-tuple-element.70), channel_id=1, source_target_pairs={{0,2},{1,3},{2,0},{3,1},{4,6},{5,7},{6,4},{7,5},{8,10},{9,11},{10,... | collective-permute-start | bytes 393224 | tf_op jit(solution)/shard_map/ppermute | solution.py:208
  191.0 9.5 %collective-permute-start.11 = (f32[128,256]{1,0:T(8,128)S(1)}, f32[128,256]{1,0:T(8,128)S(1)}, u32[]{:S(2)}, u32[]{:S(2)}) collective-permute-start(f32[128,256]{1,0:T(8,128)S(1)} %get-tuple-element.71), channel_id=1, source_target_pairs={{0,3},{1,0},{2,1},{3,2},{4,7},{5,4},{6,5},{7,6},{8,11},{9,8},{10,9... | collective-permute-start | bytes 393224 | tf_op jit(solution)/shard_map/ppermute | solution.py:208
  (1 other events, 1.1 us)
Sparse Core Ops, SparseCore 0:
  45.7 64.5 all-gather.1
